TPU v7x, 512 devices: a whole 4x8x8 slice. The times are simulated.
512 devices in a mesh: lon: 32 (over z_lo, y, core), ch: 16 (over x, z_hi).
Axes of the slice: x: 4, y: 8, z: 8 (z_hi: 4, z_lo: 2; z = z_hi * 2 + z_lo), core: 2. Of those that a mesh axis runs over, the one named last changes fastest.
Arguments:
- grid_state: bfloat16 [128, 512, 1024], P(None, 'lon', 'ch'), may hold values from -40 to 40
- first_gain: bfloat16 [1024], P('ch'), may hold values from 0.099609375 to 1.8984375
- spectral_first: bfloat16 [2, 1024, 64], P(None, 'ch'), may hold values from -0.5 to 0.5
- spectral_second: bfloat16 [2, 1024, 64], P(None, 'ch'), may hold values from -0.5 to 0.5
- second_gain: bfloat16 [1024], P('ch'), may hold values from 0.099609375 to 1.8984375
- up_weight: bfloat16 [1024, 4096], P(None, 'ch'), may hold values from -0.1875 to 0.1875
- down_weight: bfloat16 [4096, 1024], P('ch'), may hold values from -0.125 to 0.125
Outputs:
- block_out: bfloat16 [128, 512, 1024], P(None, 'lon', 'ch')
All inputs are finite; a program needn't handle non-finite values.
Results may differ from a plain program's by a relative error of at most 0.015.
Values may be sent and summed in bfloat16 or wider, within the bound.
No kernel may reach another device: no remote copies, remote signals or barrier semaphores. Data moves between devices by JAX's collectives and lax.ppermute only.
A program may use at most 64 MiB of HBM per device.

v0:
```python
import math

import jax
import jax.numpy as jnp
from jax import lax
from jax.sharding import PartitionSpec as P

H = 128
W = 512
C = 1024
KW = 256


EPSILON = 1e-05
THRESHOLD = 0.1
HIGHEST = lax.Precision.HIGHEST


def dft_tables(length, harmonics):
    sample_idx = jnp.arange(length, dtype=jnp.int32)[:, None]
    harmonic_idx = jnp.arange(harmonics, dtype=jnp.int32)[None, :]
    phase = (sample_idx * harmonic_idx % length).astype(jnp.float32) * (2.0 * math.pi / length)
    factor = 1.0 / math.sqrt(length)
    return (jnp.cos(phase) * factor, jnp.sin(phase) * factor)


def normalize(values, total, square, gain, width):
    centre = total[..., None] / width
    spread = square[..., None] / width - centre * centre
    return ((values - centre) * lax.rsqrt(spread + EPSILON) * gain).astype(jnp.bfloat16)


def soft_shrink(values):
    return values - jnp.clip(values, -THRESHOLD, THRESHOLD)


def lat_apply(values, table):
    return jnp.einsum("kch,hq->kcq", values, table, precision=HIGHEST)


def complex_mix(real_part, imag_part, weight):
    mode_len, chan_len, lat_len = real_part.shape
    block_width = weight.shape[-1]
    blocks = chan_len // block_width
    w_real = weight[0].reshape(blocks, block_width, block_width)
    w_imag = weight[1].reshape(blocks, block_width, block_width)
    real_blocks = real_part.reshape(mode_len, blocks, block_width, lat_len)
    imag_blocks = imag_part.reshape(mode_len, blocks, block_width, lat_len)

    def product(left, right):
        return jnp.einsum("knbq,nbd->kndq", left, right, preferred_element_type=jnp.float32)

    new_real = product(real_blocks, w_real) - product(imag_blocks, w_imag)
    new_imag = product(real_blocks, w_imag) + product(imag_blocks, w_real)
    return (
        new_real.reshape(mode_len, chan_len, lat_len),
        new_imag.reshape(mode_len, chan_len, lat_len),
    )


def per_device(
    grid_state, first_gain, spectral_first, spectral_second, second_gain, up_weight, down_weight
):
    lat_count, col_count, chan_count = grid_state.shape
    values = grid_state.astype(jnp.float32)
    total_one, square_one = lax.psum(
        (jnp.sum(values, axis=2), jnp.sum(values * values, axis=2)), "ch"
    )
    normed_first = normalize(values, total_one, square_one, first_gain, C)
    columns = lax.all_to_all(normed_first, "lon", split_axis=2, concat_axis=1, tiled=True)
    lon_cos, lon_sin = dft_tables(W, KW)
    lat_cos, lat_sin = dft_tables(H, H)
    column_data = columns.astype(jnp.float32)
    fwd_real = jnp.einsum("hwc,wk->kch", column_data, lon_cos, precision=HIGHEST)
    fwd_imag = -jnp.einsum("hwc,wk->kch", column_data, lon_sin, precision=HIGHEST)
    spec_real = lat_apply(fwd_real, lat_cos) + lat_apply(fwd_imag, lat_sin)
    spec_imag = lat_apply(fwd_imag, lat_cos) - lat_apply(fwd_real, lat_sin)
    modes = lax.all_to_all(
        jnp.stack([spec_real, spec_imag]).astype(jnp.bfloat16),
        "lon",
        split_axis=1,
        concat_axis=2,
        tiled=True,
    )
    mid_real, mid_imag = complex_mix(modes[0], modes[1], spectral_first)
    mid_real = jax.nn.relu(mid_real).astype(jnp.bfloat16)
    mid_imag = jax.nn.relu(mid_imag).astype(jnp.bfloat16)
    out_real, out_imag = complex_mix(mid_real, mid_imag, spectral_second)
    out_real = soft_shrink(out_real)
    out_imag = soft_shrink(out_imag)
    inv_real = lat_apply(out_real, lat_cos) - lat_apply(out_imag, lat_sin)
    inv_imag = lat_apply(out_imag, lat_cos) + lat_apply(out_real, lat_sin)
    returned = lax.all_to_all(
        jnp.stack([inv_real, inv_imag]).astype(jnp.bfloat16),
        "lon",
        split_axis=2,
        concat_axis=1,
        tiled=True,
    ).astype(jnp.float32)
    back_real = returned[0]
    back_imag = returned[1]
    harmonic_weight = jnp.where(jnp.arange(KW, dtype=jnp.int32) == 0, 1.0, 2.0).astype(jnp.float32)
    inv_cos = lon_cos * harmonic_weight[None, :]
    inv_sin = lon_sin * harmonic_weight[None, :]
    grid_cols = jnp.einsum("kch,wk->hwc", back_real, inv_cos, precision=HIGHEST)
    grid_cols = grid_cols - jnp.einsum("kch,wk->hwc", back_imag, inv_sin, precision=HIGHEST)
    filtered = lax.all_to_all(
        grid_cols.astype(jnp.bfloat16), "lon", split_axis=1, concat_axis=2, tiled=True
    )
    mixed = (values + normed_first.astype(jnp.float32) + filtered.astype(jnp.float32)).astype(
        jnp.bfloat16
    )
    mixed_wide = mixed.astype(jnp.float32)
    token_count = lat_count * col_count
    everything, whole_gain = (
        lax.all_gather(mixed, "ch", axis=2, tiled=True),
        lax.all_gather(second_gain, "ch", axis=0, tiled=True),
    )
    spread_all = everything.astype(jnp.float32)
    normed_second = normalize(
        spread_all,
        jnp.sum(spread_all, axis=2),
        jnp.sum(spread_all * spread_all, axis=2),
        whole_gain,
        C,
    )
    upward = jnp.dot(
        normed_second.reshape(token_count, C), up_weight, preferred_element_type=jnp.float32
    )
    hidden = jax.nn.gelu(upward).astype(jnp.bfloat16)
    summed = lax.psum_scatter(
        jnp.einsum("tj,jc->ct", hidden, down_weight, preferred_element_type=jnp.float32).astype(
            jnp.bfloat16
        ),
        "ch",
        scatter_dimension=0,
        tiled=True,
    ).astype(jnp.float32)
    branch = summed.T.reshape(lat_count, col_count, chan_count)
    return (mixed_wide + branch).astype(jnp.bfloat16)


def solution(mesh):
    return jax.shard_map(
        per_device,
        mesh=mesh,
        in_specs=(
            P(None, "lon", "ch"),
            P("ch"),
            P(None, "ch", None),
            P(None, "ch", None),
            P("ch"),
            P(None, "ch"),
            P("ch", None),
        ),
        out_specs=P(None, "lon", "ch"),
        check_vma=False,
    )
```

profile of v0, /device:TPU:1, one launch (start us, length us, event | category | flops | bytes accessed | tf_op | source)
XLA Modules:
  0.0 401.5 jit_solution(9092841457983095221)
XLA Ops:
  6.5 1.2 convert_reduce_fusion.1
  8.4 74.7 %all-reduce.1 = (f32[128,16]{0,1:T(8,128)S(1)}, f32[128,16]{0,1:T(8,128)S(1)}) all-reduce(f32[128,16]{0,1:T(8,128)S(1)} %get-tuple-element.8, f32[128,16]{0,1:T(8,128)S(1)} %get-tuple-element.7), channel_id=1, replica_groups=mesh['lon'=32,'ch'=16] {'ch'}, use_global_device_ids=true, to_apply=%region_3.0 | all-reduce | flops 4096 | bytes 32768 | tf_op jit(solution)/shard_map/psum | solution.py:66
  83.0 1.1 fusion.41
  84.2 34.5 %all_to_all.57 = bf16[128,16,64]{0,1,2:T(8,128)(2,1)S(1)} all-to-all(bf16[128,16,64]{0,1,2:T(8,128)(2,1)S(1)} %fusion.41), channel_id=1, replica_groups=mesh['lon'=32,'ch'=16] {'lon'}, dimensions={2} | all-to-all | bytes 524288 | tf_op jit(solution)/shard_map/all_to_all | solution.py:70
  118.8 2.7 convolution_bitcast_fusion
  121.4 2.7 fusion.17
  127.0 16.2 %all_to_all.58 = bf16[2,256,2,128]{3,2,0,1:T(2,128)(2,1)S(1)} all-to-all(bf16[2,256,2,128]{3,2,0,1:T(2,128)(2,1)S(1)} %copy.123), channel_id=1, replica_groups=mesh['lon'=32,'ch'=16] {'lon'}, dimensions={1} | all-to-all | bytes 524288 | tf_op jit(solution)/shard_map/all_to_all | solution.py:78
  147.8 0.9 copy.129
  148.7 5.0 %all-to-all-start.2 = ((bf16[2,8,64,128]{3,1,0,2:T(8,128)(2,1)}), bf16[2,8,64,128]{3,1,0,2:T(8,128)(2,1)S(1)}, u32[]{:S(2)}, u32[]{:S(2)}) async-start(bf16[2,8,64,128]{3,1,0,2:T(8,128)(2,1)} %copy.129), calls=%async_computation.2 | async-start | bytes 524288 | tf_op jit(solution)/shard_map/all_to_all | solution.py:93
  154.0 11.8 %all-to-all-done.2 = bf16[2,8,64,128]{3,1,0,2:T(8,128)(2,1)S(1)} async-done(((bf16[2,8,64,128]{3,1,0,2:T(8,128)(2,1)}), bf16[2,8,64,128]{3,1,0,2:T(8,128)(2,1)S(1)}, u32[]{:S(2)}, u32[]{:S(2)}) %all-to-all-start.2) | async-done | bytes 262176 | tf_op jit(solution)/shard_map/all_to_all | solution.py:93
  165.8 2.3 fusion.48
  168.1 2.5 fusion.18
  170.9 16.2 %all_to_all.59 = bf16[128,512,2]{0,2,1:T(2,128)(2,1)S(1)} all-to-all(bf16[128,512,2]{0,2,1:T(2,128)(2,1)S(1)} %copy.131), channel_id=1, replica_groups=mesh['lon'=32,'ch'=16] {'lon'}, dimensions={1} | all-to-all | bytes 524288 | tf_op jit(solution)/shard_map/all_to_all | solution.py:107
  187.3 0.9 fusion.44
  188.3 1.3 dynamic-slice
  190.4 32.4 %all-reduce = bf16[1024]{0:T(1024)(128)(2,1)S(1)} all-reduce(bf16[1024]{0:T(1024)(128)(2,1)S(1)} %dynamic-update-slice), channel_id=1, replica_groups=mesh['lon'=32,'ch'=16] {'ch'}, use_global_device_ids=true, to_apply=%add | all-reduce | flops 1024 | bytes 4096
  222.8 37.9 %all-gather.2.cloned.1.call-done = bf16[128,16,1024]{0,1,2:T(8,128)(2,1)} async-done(((bf16[128,16,64]{0,1,2:T(8,128)(2,1)}), bf16[128,16,1024]{0,1,2:T(8,128)(2,1)}) %all-gather.2.cloned.1.call-update) | async-done | bytes 4194320 | tf_op jit(solution)/shard_map/all_gather | solution.py:116
  260.7 7.4 %copy.134 = bf16[128,16,1024]{2,1,0:T(8,128)(2,1)} copy(bf16[128,16,1024]{0,1,2:T(8,128)(2,1)} %all-gather.2.cloned.1.call-done) | data formatting | bytes 8388608 | tf_op jit(solution)/shard_map/all_gather | solution.py:116
  268.2 3.6 convert_reduce_fusion
  272.1 4.4 %fusion.2 = bf16[128,16,1024]{2,1,0:T(8,128)(2,1)} fusion(bf16[128,16,1024]{2,1,0:T(8,128)(2,1)} %copy.134, f32[1024]{0:T(1024)S(1)} %convert_element_type.123, f32[128,16]{1,0:T(8,128)S(1)} %copy.138, f32[128,16]{1,0:T(8,128)S(1)} %copy.136), kind=kLoop, calls=%fused_computation.5 | loop fusion | flops 10485760 | bytes 8409088 | tf_op jit(solution)/shard_map/convert_element_type | solution.py:30
  276.5 8.5 %convert_bitcast_fusion = bf16[1024,2048]{0,1:T(8,128)(2,1)} fusion(bf16[256,1024]{1,0:T(8,128)(2,1)S(1)} %copy-done, bf16[2048,1024]{1,0:T(8,128)(2,1)} %bitcast.168, bf16[1024,256]{1,0:T(8,128)(2,1)S(1)} %copy-done.5), kind=kOutput, calls=%fused_computation.7 | convolution fusion | flops 2154299392 | bytes 9437184 | tf_op jit(solution)/shard_map/tj,jc->ct/dot_general | solution.py:132
  284.9 6.5 %copy.147 = bf16[1024,2048]{1,0:T(8,128)(2,1)} copy(bf16[1024,2048]{0,1:T(8,128)(2,1)} %convert_bitcast_fusion) | data formatting | bytes 8388608
  291.5 100.5 %reduce-scatter.4.cloned.1.call-done = bf16[64,2048]{1,0:T(8,128)(2,1)} async-done(((bf16[1024,2048]{1,0:T(8,128)(2,1)}), bf16[64,2048]{1,0:T(8,128)(2,1)}) %reduce-scatter.4.cloned.1.call-update) | async-done | bytes 262160
  392.0 1.2 copy.148
  (60 shorter events, 10.9 us)
Async XLA Ops:
  6.5 269.9 %copy-start = (bf16[256,1024]{1,0:T(8,128)(2,1)S(1)}, bf16[256,1024]{1,0:T(8,128)(2,1)}, u32[]{:S(2)}) copy-start(bf16[256,1024]{1,0:T(8,128)(2,1)} %param.13) | copy-start | bytes 1572868
  121.4 22.1 %copy-start.3 = (bf16[2,64,64]{2,1,0:T(8,128)(2,1)S(1)}, bf16[2,64,64]{2,1,0:T(8,128)(2,1)}, u32[]{:S(2)}) copy-start(bf16[2,64,64]{2,1,0:T(8,128)(2,1)} %param.9) | copy-start | bytes 49156
  121.4 22.8 %copy-start.4 = (bf16[2,64,64]{2,1,0:T(8,128)(2,1)S(1)}, bf16[2,64,64]{2,1,0:T(8,128)(2,1)}, u32[]{:S(2)}) copy-start(bf16[2,64,64]{2,1,0:T(8,128)(2,1)} %param.10) | copy-start | bytes 49156
  148.7 17.1 %all-to-all-start.2 = ((bf16[2,8,64,128]{3,1,0,2:T(8,128)(2,1)}), bf16[2,8,64,128]{3,1,0,2:T(8,128)(2,1)S(1)}, u32[]{:S(2)}, u32[]{:S(2)}) async-start(bf16[2,8,64,128]{3,1,0,2:T(8,128)(2,1)} %copy.129), calls=%async_computation.2 | async-start | bytes 524288 | tf_op jit(solution)/shard_map/all_to_all | solution.py:93
  153.7 107.0 %all-gather.2.cloned.1.call-start = ((), (), s32[]{:S(2)}) async-start(), calls=%async_computation.5 | async-start | bytes 4456448 | tf_op jit(solution)/shard_map/all_gather | solution.py:116
  165.8 21.4 %copy-start.1 = (bf16[128,16,64]{0,2,1:T(8,128)(2,1)S(1)}, bf16[128,16,64]{0,2,1:T(8,128)(2,1)}, u32[]{:S(2)}) copy-start(bf16[128,16,64]{0,2,1:T(8,128)(2,1)} %param.7) | copy-start | bytes 786436
  168.1 22.1 %copy-start.6 = (bf16[64]{0:T(256)(128)(2,1)S(1)}, bf16[64]{0:T(256)(128)(2,1)}, u32[]{:S(2)}) copy-start(bf16[64]{0:T(256)(128)(2,1)} %param.11) | copy-start | bytes 388
  188.2 203.8 %reduce-scatter.4.cloned.1.call-start = ((), (), s32[]{:S(2)}) async-start(), calls=%async_computation.6 | async-start | bytes 4456448
  272.1 4.4 %copy-start.5 = (bf16[1024,256]{1,0:T(8,128)(2,1)S(1)}, bf16[1024,256]{1,0:T(8,128)(2,1)}, u32[]{:S(2)}) copy-start(bf16[1024,256]{1,0:T(8,128)(2,1)} %param.12) | copy-start | bytes 1572868
  291.5 102.4 %copy-start.2 = (bf16[128,16,64]{0,1,2:T(8,128)(2,1)S(1)}, bf16[128,16,64]{0,1,2:T(8,128)(2,1)}, u32[]{:S(2)}) copy-start(bf16[128,16,64]{0,1,2:T(8,128)(2,1)} %fusion.44) | copy-start | bytes 786436
Sparse Core Ops, SparseCore 0:
  188.3 72.3 all-gather.1
  291.6 100.3 reduce-scatter.3
where the time goes:
time: 402 us
  blocking collectives  174 us (43%)
  waiting for transfers between devices  150 us (37%)
  matrix products  25.2 us (6%)
  local copies, waits for them, and re-layouts  20.4 us (5%)
  between operations  14.4 us (4%)
  other arithmetic  12.1 us (3%)
  starting transfers between devices  5.27 us (1%)
    unnamed x3, waiting for transfers between devices  101 us
    psum x1, blocking collectives, per_device(): lax.psum((jnp.sum(values, axis=2), jnp.sum(values * values, axis=2)), 'ch')  74.7 us
    all_gather x1, waiting for transfers between devices, per_device(): lax.all_gather(mixed, 'ch', axis=2, tiled=True)  37.9 us
    all_to_all x1, blocking collectives, per_device(): lax.all_to_all(normed_first, 'lon', split_axis=2, concat_axis=1, tiled=True)  34.5 us
    unnamed x1, blocking collectives  32.4 us
    all_to_all x1, blocking collectives, per_device(): lax.all_to_all(grid_cols.astype(jnp.bfloat16), 'lon', split_axis=1, conca...  16.2 us
    all_to_all x1, blocking collectives, per_device(): lax.all_to_all(jnp.stack([spec_real, spec_imag]).astype(jnp.bfloat16), 'l...  16.2 us
    all_to_all x1, waiting for transfers between devices, per_device(): lax.all_to_all(jnp.stack([inv_real, inv_imag]).astype(jnp.bfloat16), 'lon...  11.8 us
  transfers between devices with their start and end apart: 3, of which 3 were waited for; matrix products, arithmetic and copies ran while one was open for 0% of the time, Pallas kernels for 0%

commit v1 on v0

v1 whole, which is shorter than its diff:
```python
import math

import jax
import jax.numpy as jnp
import numpy as np
from jax import lax
from jax.sharding import Mesh
from jax.sharding import PartitionSpec as P

EPSILON = 1e-05
THRESHOLD = 0.1
LAT = 128
LON = 512
KW = 256
C = 1024
F32 = jnp.float32
BF16 = jnp.bfloat16

LON_AXES = ("zl", "y", "core")
QUAD = ("zl", "core")


def lat_table():
    lat = np.arange(LAT)
    rows = np.zeros((LAT, LAT))
    for mode in range(LAT // 2):
        phase = 2.0 * math.pi * ((lat * mode) % LAT) / LAT
        rows[2 * mode] = np.cos(phase)
        rows[2 * mode + 1] = np.sin(phase)
    rows[1] = np.cos(math.pi * lat)
    return rows / math.sqrt(LAT)


def lon_table():
    phase = 2.0 * math.pi * ((np.arange(KW)[:, None] * np.arange(LON)[None, :]) % LON) / LON
    return np.concatenate([np.cos(phase), np.sin(phase)]) / math.sqrt(LON)


def lon_inverse_table():
    weight = np.where(np.arange(KW) == 0, 1.0, 2.0)
    return lon_table().T * np.concatenate([weight, weight])[None, :]


def shrink(values):
    return values - jnp.clip(values, -THRESHOLD, THRESHOLD)


def mix_tables(first, second, special):
    wr, wi = first[0], first[1]
    zero = jnp.zeros_like(wr)
    plain = jnp.concatenate(
        [
            jnp.concatenate([wr, wi, wr, wi], axis=1),
            jnp.concatenate([wi, -wr, -wi, wr], axis=1),
            jnp.concatenate([wi, -wr, wi, -wr], axis=1),
            jnp.concatenate([-wr, -wi, wr, wi], axis=1),
        ]
    )
    edge = jnp.concatenate(
        [
            jnp.concatenate([wr, wi, zero, zero], axis=1),
            jnp.concatenate([zero, zero, wr, wi], axis=1),
            jnp.concatenate([wi, -wr, zero, zero], axis=1),
            jnp.concatenate([zero, zero, wi, -wr], axis=1),
        ]
    )
    vr, vi = second[0], second[1]
    none = jnp.zeros((128, 64), vr.dtype)
    real = jnp.concatenate([vr, -vi])
    imag = jnp.concatenate([vi, vr])

    def columns(pieces):
        return jnp.concatenate(
            [jnp.concatenate([top, bottom]) for top, bottom in pieces], axis=1
        )

    plain_out = columns(
        [
            (real, none),
            (-imag, none),
            (none, real),
            (none, imag),
            (-imag, none),
            (-real, none),
            (none, -imag),
            (none, real),
        ]
    )
    edge_out = columns(
        [
            (real, none),
            (none, real),
            (none, none),
            (none, none),
            (-imag, none),
            (none, -imag),
            (none, none),
            (none, none),
        ]
    )
    mix_in = jnp.stack([jnp.where(special, edge, plain), plain])
    mix_out = jnp.stack([jnp.where(special, edge_out, plain_out), plain_out])
    return mix_in, mix_out


def per_device(grid_state, first_gain, spectral_first, spectral_second, second_gain, up_weight, down_weight):
    quarter = lax.axis_index("zl") * 2 + lax.axis_index("core")
    special = (lax.axis_index("zl") + lax.axis_index("y") + lax.axis_index("core")) == 0
    part = up_weight.shape[1] // 4
    up_part = lax.dynamic_slice_in_dim(up_weight, quarter * part, part, axis=1).T
    down_part = lax.dynamic_slice_in_dim(down_weight, quarter * part, part, axis=0)
    weights = lax.all_gather(jnp.stack([up_part, down_part]), "ch", axis=0)

    tokens = grid_state.transpose(1, 2, 0)
    values = tokens.astype(F32)
    gain_row = jnp.pad(second_gain.astype(F32), (0, 64))[None]
    sums = jnp.concatenate([jnp.sum(values, axis=1), jnp.sum(values * values, axis=1), gain_row])
    sums = jnp.pad(sums, ((0, 7), (0, 0)))
    sums = lax.all_to_all(jnp.broadcast_to(sums[None], (16, 40, 128)), "ch", 0, 0)
    second_all = sums[:, 32, :64].reshape(C, 1)
    sums = jnp.sum(sums[:, :32], axis=0)
    centre = sums[:16] / C
    spread = sums[16:] / C - centre * centre
    scale = lax.rsqrt(spread + EPSILON)
    normed = (
        (values - centre[:, None]) * scale[:, None] * first_gain.astype(F32)[None, :, None]
    ).astype(BF16)

    table = jnp.asarray(lat_table().reshape(32, 4, LAT), BF16)
    rows = jnp.einsum("lqh,wch->lwqc", table, normed, preferred_element_type=F32)
    rows = rows.astype(BF16).reshape(32, 16, 256)
    rows = lax.all_to_all(rows, LON_AXES, 0, 0).reshape(LON, 256)

    waves = jnp.dot(jnp.asarray(lon_table(), BF16), rows, preferred_element_type=F32).astype(BF16)
    mix_in, mix_out = mix_tables(spectral_first, spectral_second, special)
    outs = []
    for pair in range(2):
        lanes = slice(pair * 128, pair * 128 + 128)
        middle = jnp.dot(waves[:KW, lanes], mix_in[pair, :128], preferred_element_type=F32)
        middle += jnp.dot(waves[KW:, lanes], mix_in[pair, 128:], preferred_element_type=F32)
        middle = jax.nn.relu(middle).astype(BF16)
        mixed_modes = shrink(jnp.dot(middle, mix_out[pair], preferred_element_type=F32))
        outs.append(
            jnp.concatenate(
                [
                    mixed_modes[:, :128] + mixed_modes[:, 128:256],
                    mixed_modes[:, 256:384] + mixed_modes[:, 384:],
                ]
            ).astype(BF16)
        )
    modes = jnp.concatenate(outs, axis=1)
    back = jnp.dot(jnp.asarray(lon_inverse_table(), BF16), modes, preferred_element_type=F32)
    back = lax.all_to_all(back.astype(BF16).reshape(32, 16, 256), LON_AXES, 0, 0)
    filtered = jnp.einsum(
        "lqh,lwqc->wch", table, back.reshape(32, 16, 4, 64), preferred_element_type=F32
    ).astype(BF16)
    mixed = (values + normed.astype(F32) + filtered.astype(F32)).astype(BF16)

    wide = lax.all_to_all(mixed, "ch", 0, 0).reshape(C, 128).astype(F32)
    mean = jnp.sum(wide, axis=0, keepdims=True) / C
    power = jnp.sum(wide * wide, axis=0, keepdims=True) / C - mean * mean
    normed_second = ((wide - mean) * lax.rsqrt(power + EPSILON) * second_all).astype(BF16)
    group = lax.all_to_all(jnp.broadcast_to(normed_second[None], (4, C, 128)), QUAD, 0, 0)
    upward = jnp.einsum("sjd,idt->isjt", weights[:, 0], group, preferred_element_type=F32)
    hidden = jax.nn.gelu(upward).astype(BF16)
    sums_out = jnp.einsum("sjc,isjt->ict", weights[:, 1], hidden, preferred_element_type=F32)
    sums_out = lax.all_to_all(sums_out.astype(BF16), QUAD, 0, 0)
    branch = jnp.sum(sums_out.astype(F32), axis=0).astype(BF16).reshape(16, 64, 128)
    branch = lax.all_to_all(branch, "ch", 0, 0)
    return (mixed.astype(F32) + branch.astype(F32)).astype(BF16).transpose(2, 0, 1)


def solution(mesh):
    fine = Mesh(mesh.devices.reshape(2, 8, 2, 16), ("zl", "y", "core", "ch"))
    return jax.shard_map(
        per_device,
        mesh=fine,
        in_specs=(
            P(None, LON_AXES, "ch"),
            P("ch"),
            P(None, "ch", None),
            P(None, "ch", None),
            P("ch"),
            P(None, "ch"),
            P("ch", None),
        ),
        out_specs=P(None, LON_AXES, "ch"),
        check_vma=False,
    )
```

time: 402 us -> 177 us (0.44)
  the two profiles are of different devices: /device:TPU:1 before, /device:TPU:32 now
where the time goes in v1:
time: 177 us; the launch traced here: 176 us
  blocking collectives  72.3 us (41%)
  waiting for transfers between devices  46.2 us (26%)
  starting transfers between devices  24.4 us (14%)
  between operations  13.8 us (8%)
  matrix products  9.55 us (5%)
  local copies, waits for them, and re-layouts  5.55 us (3%)
  other arithmetic  4.33 us (2%)
    all_to_all x1, waiting for transfers between devices, per_device(): wide = lax.all_to_all(mixed, 'ch', 0, 0).reshape(C, 128).astype(F32)  24.8 us
    all_to_all x1, blocking collectives, per_device(): lax.all_to_all(back.astype(BF16).reshape(32, 16, 256), LON_AXES, 0, 0)  23 us
    all_to_all x1, blocking collectives, per_device(): sums_out = lax.all_to_all(sums_out.astype(BF16), QUAD, 0, 0)  16.9 us
    all_to_all x1, blocking collectives, per_device(): lax.all_to_all(jnp.broadcast_to(normed_second[None], (4, C, 128)), QUAD,...  16.9 us
    all_to_all x1, blocking collectives, per_device(): branch = lax.all_to_all(branch, 'ch', 0, 0)  15.6 us
    all_to_all x1, waiting for transfers between devices, per_device(): lax.all_to_all(jnp.broadcast_to(sums[None], (16, 40, 128)), 'ch', 0, 0)  14.7 us
    all_to_all x1, starting transfers between devices, per_device(): lax.all_to_all(jnp.broadcast_to(sums[None], (16, 40, 128)), 'ch', 0, 0)  12.9 us
    all_to_all x1, starting transfers between devices, per_device(): rows = lax.all_to_all(rows, LON_AXES, 0, 0).reshape(LON, 256)  7.92 us
  transfers between devices with their start and end apart: 4, of which 3 were waited for; matrix products, arithmetic and copies ran while one was open for 5% of the time, Pallas kernels for 0%

profile of v1, /device:TPU:32, one launch (start us, length us, event | category | flops | bytes accessed | tf_op | source)
XLA Modules:
  0.0 176.1 jit_solution(4663141497378628079)
XLA Ops:
  6.6 1.1 copy-done
  8.0 0.9 dynamic-slice_bitcast_fusion
  8.9 0.7 pad_maximum_fusion
  9.7 0.7 bitcast_convert_fusion.1
  10.4 0.7 broadcast_in_dim.13
  11.2 12.9 %all-to-all-start = ((f32[16,40,128]{2,1,0:T(8,128)}), f32[16,40,128]{2,1,0:T(8,128)S(1)}, u32[]{:S(2)}, u32[]{:S(2)}) async-start(f32[16,40,128]{2,1,0:T(8,128)} %broadcast_in_dim.13), calls=%async_computation | async-start | bytes 655360 | tf_op jit(solution)/shard_map/all_to_all | solution.py:119
  24.2 14.7 %all-to-all-done = f32[16,40,128]{2,1,0:T(8,128)S(1)} async-done(((f32[16,40,128]{2,1,0:T(8,128)}), f32[16,40,128]{2,1,0:T(8,128)S(1)}, u32[]{:S(2)}, u32[]{:S(2)}) %all-to-all-start) | async-done | bytes 327712 | tf_op jit(solution)/shard_map/all_to_all | solution.py:119
  38.9 0.5 fusion.11
  39.7 1.0 reshape.198
  40.7 7.9 %all-to-all-start.1 = ((bf16[32,16,256]{2,1,0:T(8,128)(2,1)}), bf16[32,16,256]{2,1,0:T(8,128)(2,1)S(1)}, u32[]{:S(2)}, u32[]{:S(2)}) async-start(bf16[32,16,256]{2,1,0:T(8,128)(2,1)} %reshape.198), calls=%async_computation.1 | async-start | bytes 524288 | tf_op jit(solution)/shard_map/all_to_all | solution.py:132
  49.6 6.7 %all-to-all-done.1 = bf16[32,16,256]{2,1,0:T(8,128)(2,1)S(1)} async-done(((bf16[32,16,256]{2,1,0:T(8,128)(2,1)}), bf16[32,16,256]{2,1,0:T(8,128)(2,1)S(1)}, u32[]{:S(2)}, u32[]{:S(2)}) %all-to-all-start.1) | async-done | bytes 262176 | tf_op jit(solution)/shard_map/all_to_all | solution.py:132
  56.3 0.4 fusion.16
  56.9 0.4 clamp_subtract_fusion.1
  57.5 0.4 clamp_subtract_fusion
  57.9 1.4 fusion.17
  59.5 23.0 %all_to_all.35 = bf16[32,16,256]{2,1,0:T(8,128)(2,1)S(1)} all-to-all(bf16[32,16,256]{2,1,0:T(8,128)(2,1)S(1)} %bitcast.155), channel_id=1, replica_groups=mesh['zl'=2,'y'=8,'core'=2,'ch'=16] {'zl','y','core'}, dimensions={0} | all-to-all | bytes 524288 | tf_op jit(solution)/shard_map/all_to_all | solution.py:153
  82.7 1.2 fusion.15
  83.9 3.5 %all-to-all-start.3 = ((bf16[16,64,128]{2,1,0:T(8,128)(2,1)}), bf16[16,64,128]{2,1,0:T(8,128)(2,1)S(1)}, u32[]{:S(2)}, u32[]{:S(2)}) async-start(bf16[16,64,128]{2,1,0:T(8,128)(2,1)} %fusion.15), calls=%async_computation.3 | async-start | bytes 524288 | tf_op jit(solution)/shard_map/all_to_all | solution.py:159
  87.6 24.8 %all-to-all-done.3 = bf16[16,64,128]{2,1,0:T(8,128)(2,1)S(1)} async-done(((bf16[16,64,128]{2,1,0:T(8,128)(2,1)}), bf16[16,64,128]{2,1,0:T(8,128)(2,1)S(1)}, u32[]{:S(2)}, u32[]{:S(2)}) %all-to-all-start.3) | async-done | bytes 262176 | tf_op jit(solution)/shard_map/all_to_all | solution.py:159
  112.8 16.9 %all_to_all.36 = bf16[4,1024,128]{2,1,0:T(8,128)(2,1)S(1)} all-to-all(bf16[4,1024,128]{2,1,0:T(8,128)(2,1)S(1)} %broadcast_in_dim.30), channel_id=1, replica_groups=mesh['zl'=2,'y'=8,'core'=2,'ch'=16] {'zl','core'}, dimensions={0} | all-to-all | bytes 2097152 | tf_op jit(solution)/shard_map/all_to_all | solution.py:163
  129.7 4.9 %fusion.10 = bf16[4,1024,128]{1,2,0:T(8,128)(2,1)S(1)} fusion(bf16[16,2,64,1024]{3,2,1,0:T(8,128)(2,1)} %bitcast.159, bf16[4,1024,128]{2,1,0:T(8,128)(2,1)S(1)} %all_to_all.36), kind=kOutput, calls=%fused_computation.14 | convolution fusion | flops 2152726528 | bytes 6291456 | tf_op jit(solution)/shard_map/sjc,isjt->ict/dot_general | solution.py:166
  134.7 16.9 %all_to_all.37 = bf16[4,1024,128]{1,2,0:T(8,128)(2,1)S(1)} all-to-all(bf16[4,1024,128]{1,2,0:T(8,128)(2,1)S(1)} %fusion.10), channel_id=1, replica_groups=mesh['zl'=2,'y'=8,'core'=2,'ch'=16] {'zl','core'}, dimensions={0} | all-to-all | bytes 2097152 | tf_op jit(solution)/shard_map/all_to_all | solution.py:167
  151.9 15.6 %all_to_all.38 = bf16[16,64,128]{2,1,0:T(8,128)(2,1)S(1)} all-to-all(bf16[16,64,128]{2,1,0:T(8,128)(2,1)S(1)} %bitcast.156), channel_id=1, replica_groups=mesh['zl'=2,'y'=8,'core'=2,'ch'=16] {'ch'}, dimensions={0} | all-to-all | bytes 524288 | tf_op jit(solution)/shard_map/all_to_all | solution.py:169
  167.5 1.7 fusion.38
  (54 shorter events, 3.4 us)
Async XLA Ops:
  6.5 1.2 copy-start
  6.5 32.4 %copy-start.5 = (bf16[32,4,128,1]{2,0,1,3:T(8,128)(2,1)S(1)}, bf16[32,4,128,1]{2,0,1,3:T(8,128)(2,1)}, u32[]{:S(2)}) copy-start(bf16[32,4,128,1]{2,0,1,3:T(8,128)(2,1)} %constant.78) | copy-start | bytes 98308
  6.5 3.8 %copy-start.1 = (bf16[128,16,64]{0,2,1:T(8,128)(2,1)S(1)}, bf16[128,16,64]{0,2,1:T(8,128)(2,1)}, u32[]{:S(2)}) copy-start(bf16[128,16,64]{0,2,1:T(8,128)(2,1)} %param.10) | copy-start | bytes 786436
  6.5 17.5 %copy-start.4 = (bf16[2,64,64]{2,1,0:T(8,128)(2,1)S(1)}, bf16[2,64,64]{2,1,0:T(8,128)(2,1)}, u32[]{:S(2)}) copy-start(bf16[2,64,64]{2,1,0:T(8,128)(2,1)} %param.13) | copy-start | bytes 49156
  6.5 17.6 %copy-start.6 = (bf16[64]{0:T(256)(128)(2,1)S(1)}, bf16[64]{0:T(256)(128)(2,1)}, u32[]{:S(2)}) copy-start(bf16[64]{0:T(256)(128)(2,1)} %param.11) | copy-start | bytes 388
  6.5 17.6 %copy-start.3 = (bf16[2,64,64]{2,1,0:T(8,128)(2,1)S(1)}, bf16[2,64,64]{2,1,0:T(8,128)(2,1)}, u32[]{:S(2)}) copy-start(bf16[2,64,64]{2,1,0:T(8,128)(2,1)} %param.12) | copy-start | bytes 49156
  6.6 123.2 %all-gather.3.cloned.1.call-start = ((), (), s32[]{:S(2)}) async-start(), calls=%async_computation.7 | async-start | bytes 4456448 | tf_op jit(solution)/shard_map/all_gather | solution.py:112
  11.2 27.7 %all-to-all-start = ((f32[16,40,128]{2,1,0:T(8,128)}), f32[16,40,128]{2,1,0:T(8,128)S(1)}, u32[]{:S(2)}, u32[]{:S(2)}) async-start(f32[16,40,128]{2,1,0:T(8,128)} %broadcast_in_dim.13), calls=%async_computation | async-start | bytes 655360 | tf_op jit(solution)/shard_map/all_to_all | solution.py:119
  39.7 16.6 %copy-start.2 = (bf16[512,512]{1,0:T(8,128)(2,1)S(1)}, bf16[512,512]{1,0:T(8,128)(2,1)}, u32[]{:S(2)}) copy-start(bf16[512,512]{1,0:T(8,128)(2,1)} %constant.65.clone) | copy-start | bytes 1572868
  40.7 15.6 %all-to-all-start.1 = ((bf16[32,16,256]{2,1,0:T(8,128)(2,1)}), bf16[32,16,256]{2,1,0:T(8,128)(2,1)S(1)}, u32[]{:S(2)}, u32[]{:S(2)}) async-start(bf16[32,16,256]{2,1,0:T(8,128)(2,1)} %reshape.198), calls=%async_computation.1 | async-start | bytes 524288 | tf_op jit(solution)/shard_map/all_to_all | solution.py:132
  83.9 28.4 %all-to-all-start.3 = ((bf16[16,64,128]{2,1,0:T(8,128)(2,1)}), bf16[16,64,128]{2,1,0:T(8,128)(2,1)S(1)}, u32[]{:S(2)}, u32[]{:S(2)}) async-start(bf16[16,64,128]{2,1,0:T(8,128)(2,1)} %fusion.15), calls=%async_computation.3 | async-start | bytes 524288 | tf_op jit(solution)/shard_map/all_to_all | solution.py:159
Sparse Core Ops, SparseCore 0:
  10.4 97.4 all-gather.2

commit v2 on v1

v2 whole, which is shorter than its diff:
```python
import math

import jax
import jax.numpy as jnp
import numpy as np
from jax import lax
from jax.experimental import pallas as pl
from jax.experimental.pallas import tpu as pltpu
from jax.sharding import Mesh
from jax.sharding import PartitionSpec as P

EPSILON = 1e-05
THRESHOLD = 0.1
LAT = 128
GAIN_ROW = 416
LON = 512
KW = 256
C = 1024
F32 = jnp.float32
BF16 = jnp.bfloat16
VMEM = pl.BlockSpec(memory_space=pltpu.VMEM)
PARAMS = pltpu.CompilerParams(vmem_limit_bytes=10 << 20)

LON_AXES = ("zl", "y", "core")
CH_AXES = ("xh", "xl", "zh")
OCT_AXES = ("xl", "zh")
NT = (((1,), (1,)), ((), ()))
TN = (((0,), (0,)), ((), ()))


def lat_table():
    lat = np.arange(LAT)
    rows = np.zeros((LAT, LAT))
    for mode in range(LAT // 2):
        phase = 2.0 * math.pi * ((lat * mode) % LAT) / LAT
        rows[2 * mode] = np.cos(phase)
        rows[2 * mode + 1] = np.sin(phase)
    rows[1] = np.cos(math.pi * lat)
    return rows / math.sqrt(LAT)


def lat_pairs():
    table = lat_table().reshape(32, 2, 2, LAT)
    return table.transpose(1, 0, 2, 3).reshape(64, 2 * LAT)


def lon_table():
    phase = 2.0 * math.pi * ((np.arange(KW)[:, None] * np.arange(LON)[None, :]) % LON) / LON
    return np.concatenate([np.cos(phase), np.sin(phase)]) / math.sqrt(LON)


def lon_inverse_table():
    weight = np.where(np.arange(KW) == 0, 1.0, 2.0)
    return lon_table().T * np.concatenate([weight, weight])[None, :]


SIGNS_IN = np.array(
    [
        [[1, 0, 1, 0], [0, -1, 0, 1], [0, -1, 0, -1], [-1, 0, 1, 0]],
        [[0, 1, 0, 1], [1, 0, -1, 0], [1, 0, 1, 0], [0, -1, 0, 1]],
        [[1, 0, 0, 0], [0, 0, 1, 0], [0, -1, 0, 0], [0, 0, 0, -1]],
        [[0, 1, 0, 0], [0, 0, 0, 1], [1, 0, 0, 0], [0, 0, 1, 0]],
    ]
)
SIGNS_OUT = np.array(
    [
        [
            [1, 0, 0, 0, 0, -1, 0, 0],
            [0, -1, 0, 0, -1, 0, 0, 0],
            [0, 0, 1, 0, 0, 0, 0, 1],
            [0, 0, 0, 1, 0, 0, -1, 0],
        ],
        [
            [0, -1, 0, 0, -1, 0, 0, 0],
            [-1, 0, 0, 0, 0, 1, 0, 0],
            [0, 0, 0, 1, 0, 0, -1, 0],
            [0, 0, -1, 0, 0, 0, 0, -1],
        ],
        [
            [1, 0, 0, 0, 0, 0, 0, 0],
            [0, 0, 0, 0, -1, 0, 0, 0],
            [0, 1, 0, 0, 0, 0, 0, 0],
            [0, 0, 0, 0, 0, -1, 0, 0],
        ],
        [
            [0, 0, 0, 0, -1, 0, 0, 0],
            [-1, 0, 0, 0, 0, 0, 0, 0],
            [0, 0, 0, 0, 0, -1, 0, 0],
            [0, -1, 0, 0, 0, 0, 0, 0],
        ],
    ]
)


def sign_rows(signs):
    wide = np.repeat(signs, 64, axis=2)
    return np.pad(wide, ((0, 0), (0, 4), (0, 0)))


def shrink(values):
    return values - jnp.clip(values, -THRESHOLD, THRESHOLD)


def column_of(row):
    size = row.shape[1]
    diagonal = lax.broadcasted_iota(jnp.int32, (size, size), 0) == lax.broadcasted_iota(
        jnp.int32, (size, size), 1
    )
    return jnp.sum(jnp.where(diagonal, row, 0.0), axis=1, keepdims=True)


def setup_kernel(place_ref, up_ref, down_ref, tokens_ref, gain_ref, packed_ref, sums_ref, up_part, tokens_part, gain_part, sems):
    half = pl.ds(pl.multiple_of(place_ref[0] * 128, 128), 128)
    pairs = [
        (tokens_ref, tokens_part),
        (gain_ref, gain_part),
        (up_ref.at[:, half], up_part),
        (down_ref.at[half], packed_ref.at[1]),
    ]
    copies = [pltpu.make_async_copy(a, b, sems.at[i]) for i, (a, b) in enumerate(pairs)]
    for copy in copies:
        copy.start()
    copies[0].wait()
    copies[1].wait()
    values = tokens_part[...].astype(F32)
    gain = gain_part[...].astype(F32).reshape(1, 64)
    block = jnp.concatenate(
        [
            jnp.sum(values, axis=1),
            jnp.sum(values * values, axis=1),
            jnp.broadcast_to(jnp.concatenate([gain, gain], axis=1), (8, 128)),
        ]
    )
    sums_ref[...] = jnp.broadcast_to(block[None], sums_ref.shape)
    copies[2].wait()
    row = lax.broadcasted_iota(jnp.int32, (128, 128), 0)
    lane = lax.broadcasted_iota(jnp.int32, (128, 128), 1)
    pick = jnp.where(lane == row, 1.0, 0.0).astype(BF16)
    packed_ref[0] = lax.dot_general(pick, up_part[...], NT, preferred_element_type=F32).astype(BF16)
    copies[3].wait()


def setup(*args):
    return pl.pallas_call(
        setup_kernel,
        out_shape=[shape((2, 128, C)), shape((16, 40, 128), F32)],
        in_specs=[pl.BlockSpec(memory_space=pltpu.SMEM)] + [pl.BlockSpec(memory_space=pl.ANY)] * 4,
        out_specs=[VMEM] * 2,
        scratch_shapes=[
            pltpu.VMEM((C, 128), BF16),
            pltpu.VMEM((16, 64, 128), BF16),
            pltpu.VMEM((64,), BF16),
            pltpu.SemaphoreType.DMA((4,)),
        ],
        compiler_params=pltpu.CompilerParams(vmem_limit_bytes=60 << 20),
        name="setup",
    )(*args)


def forward_kernel(sums_ref, tokens_ref, small_ref, normed_ref, out_ref, twice, wide):
    total = jnp.sum(sums_ref[:, :32, :], axis=0)
    centre = total[:16] / C
    spread = total[16:] / C - centre * centre
    scale = lax.rsqrt(spread + EPSILON)
    gain = column_of(small_ref[GAIN_ROW : GAIN_ROW + 1, :64].astype(F32))
    twice[...] = jnp.zeros_like(twice)
    table = small_ref[:64]
    for w in range(16):
        values = tokens_ref[w].astype(F32)
        normed = ((values - centre[w : w + 1]) * scale[w : w + 1] * gain).astype(BF16)
        normed_ref[w] = normed
        slot = w % 2
        twice[slot, :64, :LAT] = normed
        twice[slot, 64:, LAT:] = normed
        rows = lax.dot_general(table, twice[slot], NT, preferred_element_type=F32)
        wide[:, w, :128] = rows[:32]
        wide[:, w, 128:] = rows[32:]
    out_ref[...] = wide[...].astype(BF16)


def spectral_kernel(place_ref, rows_ref, lon_ref, inverse_ref, small_ref, out_ref, modes):
    waves = jnp.dot(lon_ref[...], rows_ref[...], preferred_element_type=F32).astype(BF16)
    row = lax.broadcasted_iota(jnp.int32, (256, 8), 0) // 64
    spot = lax.broadcasted_iota(jnp.int32, (256, 8), 1)
    blocks = jnp.where(row == spot, 1.0, 0.0).astype(BF16)
    down64 = lax.broadcasted_iota(jnp.int32, (256, 64), 0) % 64
    stack = jnp.where(down64 == lax.broadcasted_iota(jnp.int32, (256, 64), 1), 1.0, 0.0).astype(BF16)

    def tables(weights, signs, columns):
        lane = lax.broadcasted_iota(jnp.int32, (64, columns), 1) % 64
        spread = jnp.where(lane == lax.broadcasted_iota(jnp.int32, (64, columns), 0), 1.0, 0.0)
        spread = spread.astype(BF16)
        tiles = []
        for part in range(2):
            tall = jnp.dot(stack, weights[part], preferred_element_type=F32).astype(BF16)
            tiles.append(jnp.dot(tall, spread, preferred_element_type=F32))
        found = []
        for kind in (0, 2):
            mask = [
                jnp.dot(blocks, signs[kind + part], preferred_element_type=F32)
                for part in range(2)
            ]
            found.append(tiles[0] * mask[0] + tiles[1] * mask[1])
        plain, edge = found
        return [jnp.where(place_ref[1] == 1, edge, plain).astype(BF16), plain.astype(BF16)]

    def rows_of(start, count):
        return small_ref[start : start + count]

    first = [rows_of(160 + 64 * part, 64)[:, :64] for part in range(2)]
    second = [rows_of(288 + 64 * part, 64)[:, :64] for part in range(2)]
    signs_in = [rows_of(64 + 8 * kind, 8) for kind in range(4)]
    signs_out = [
        jnp.concatenate([rows_of(96 + 8 * kind, 8), rows_of(128 + 8 * kind, 8)], axis=1)
        for kind in range(4)
    ]
    mix_in = tables(first, signs_in, 256)
    mix_out = tables(second, signs_out, 512)
    for pair in range(2):
        lanes = slice(pair * 128, pair * 128 + 128)
        middle = jnp.dot(waves[:KW, lanes], mix_in[pair][:128], preferred_element_type=F32)
        middle += jnp.dot(waves[KW:, lanes], mix_in[pair][128:], preferred_element_type=F32)
        middle = jnp.maximum(middle, 0.0).astype(BF16)
        back = shrink(jnp.dot(middle, mix_out[pair], preferred_element_type=F32))
        modes[:KW, lanes] = (back[:, :128] + back[:, 128:256]).astype(BF16)
        modes[KW:, lanes] = (back[:, 256:384] + back[:, 384:]).astype(BF16)
    out_ref[...] = jnp.dot(inverse_ref[...], modes[...], preferred_element_type=F32).astype(BF16)


def inverse_kernel(rows_ref, tokens_ref, normed_ref, small_ref, mixed_ref, wide):
    wide[...] = rows_ref[...].astype(F32)
    table = small_ref[:64]
    for w in range(16):
        rows = jnp.concatenate([wide[:, w, :128], wide[:, w, 128:]]).astype(BF16)
        both = lax.dot_general(rows, table, TN, preferred_element_type=F32)
        filtered = (both[:64, :LAT] + both[64:, LAT:]).astype(BF16).astype(F32)
        mixed = tokens_ref[w].astype(F32) + normed_ref[w].astype(F32) + filtered
        mixed_ref[w] = mixed.astype(BF16)


def second_norm_kernel(place_ref, own_ref, other_ref, sums_ref, out_ref, both):
    xh = place_ref[2]
    for w in range(2):
        for d in range(8):
            mine = pl.ds(pl.multiple_of(xh * 512 + d * 64, 64), 64)
            theirs = pl.ds(pl.multiple_of((1 - xh) * 512 + d * 64, 64), 64)
            both[mine, w * 128 : w * 128 + 128] = own_ref[d, w].astype(F32)
            both[theirs, w * 128 : w * 128 + 128] = other_ref[d, w].astype(F32)
    wide = both[...]
    mean = jnp.sum(wide, axis=0, keepdims=True) / C
    power = jnp.sum(wide * wide, axis=0, keepdims=True) / C - mean * mean
    scale = lax.rsqrt(power + EPSILON)
    for block in range(16):
        rows = slice(block * 64, block * 64 + 64)
        gain = column_of(sums_ref[block, 32:33, :64])
        out_ref[rows] = ((both[rows] - mean) * scale * gain).astype(BF16)


def mlp_kernel(*refs):
    pieces = refs[:8]
    own_ref, other_ref, own_out, other_out = refs[8:]
    group = jnp.concatenate([own_ref[...], other_ref[...]], axis=1)
    total = None
    for first, second in zip(pieces[0::2], pieces[1::2]):
        up = jnp.concatenate([first[0], second[0]])
        down = jnp.concatenate([first[1], second[1]])
        upward = jnp.dot(up, group, preferred_element_type=F32)
        hidden = jax.nn.gelu(upward).astype(BF16)
        found = lax.dot_general(down, hidden, TN, preferred_element_type=F32)
        total = found if total is None else total + found
    own_out[...] = total[:, :256]
    other_out[...] = total[:, 256:].astype(BF16)


def core_sum_kernel(place_ref, own_ref, other_ref, keep_ref, send_ref):
    xh = place_ref[2]
    mine = pl.ds(pl.multiple_of(xh * 512, 512), 512)
    theirs = pl.ds(pl.multiple_of((1 - xh) * 512, 512), 512)
    keep_ref[...] = own_ref[mine] + other_ref[mine].astype(F32)
    send_ref[...] = (own_ref[theirs] + other_ref[theirs].astype(F32)).astype(BF16)


def finish_kernel(mixed_ref, keep_ref, other_ref, out_ref):
    for d in range(8):
        rows = slice(d * 64, d * 64 + 64)
        branch = keep_ref[rows] + other_ref[rows].astype(F32)
        for w in range(2):
            sums = mixed_ref[d, w].astype(F32) + branch[:, w * 128 : w * 128 + 128]
            out_ref[d, w] = sums.astype(BF16)


def call(kernel, shapes, scratch, name, args, scalars=0, limit=10 << 20):
    specs = [pl.BlockSpec(memory_space=pltpu.SMEM)] * scalars + [VMEM] * (len(args) - scalars)
    many = isinstance(shapes, list)
    return pl.pallas_call(
        kernel,
        out_shape=shapes,
        in_specs=specs,
        out_specs=[VMEM] * len(shapes) if many else VMEM,
        scratch_shapes=scratch,
        compiler_params=pltpu.CompilerParams(vmem_limit_bytes=limit),
        name=name,
    )(*args)


def shape(dims, kind=BF16):
    return jax.ShapeDtypeStruct(dims, kind)


def swap(values, axis):
    return lax.ppermute(values, axis, [(0, 1), (1, 0)])


def next_pair(values):
    pairs = []
    for zh in range(4):
        pairs.append((4 + zh, (zh + 1) % 4))
        pairs.append((zh, 4 + (zh - 1) % 4))
    return lax.ppermute(values, ("zl", "zh"), pairs)


def per_device(grid_state, first_gain, spectral_first, spectral_second, second_gain, up_weight, down_weight):
    zl, core = lax.axis_index("zl"), lax.axis_index("core")
    edge = (zl + lax.axis_index("y") + core) == 0
    place = jnp.stack([core, edge.astype(jnp.int32), lax.axis_index("xh")])
    tokens = grid_state.transpose(1, 2, 0)
    packed, sums = setup(place, up_weight, down_weight, tokens, second_gain)
    z0 = next_pair(packed)
    x0 = swap(packed, "xl")
    sums = lax.all_to_all(sums, CH_AXES, 0, 0)
    signs_out = sign_rows(SIGNS_OUT).reshape(32, 512)
    small = jnp.concatenate(
        [
            jnp.asarray(lat_pairs(), BF16),
            jnp.asarray(sign_rows(SIGNS_IN).reshape(32, 256), BF16),
            jnp.asarray(signs_out[:, :256], BF16),
            jnp.asarray(signs_out[:, 256:], BF16),
            jnp.pad(spectral_first.reshape(128, 64), ((0, 0), (0, 192))),
            jnp.pad(spectral_second.reshape(128, 64), ((0, 0), (0, 192))),
            jnp.pad(first_gain[None], ((0, 15), (0, 192))),
        ]
    )
    sums, small, z0, x0 = lax.optimization_barrier((sums, small, z0, x0))
    normed, rows = call(
        forward_kernel,
        [shape((16, 64, 128)), shape((32, 16, 256))],
        [pltpu.VMEM((2, 128, 256), BF16), pltpu.VMEM((32, 16, 256), F32)],
        "norm_latitude",
        (sums, tokens, small),
    )
    rows, z0 = lax.optimization_barrier((rows, z0))
    z1 = swap(z0, "zl")
    x1 = swap(z0, "xl")
    rows = lax.all_to_all(rows, LON_AXES, 0, 0)
    rows, z1, x1 = lax.optimization_barrier((rows, z1, x1))
    back = call(
        spectral_kernel,
        shape((LON, 256)),
        [pltpu.VMEM((LON, 256), BF16)],
        "spectral",
        (
            place,
            rows.reshape(LON, 256),
            jnp.asarray(lon_table(), BF16),
            jnp.asarray(lon_inverse_table(), BF16),
            small,
        ),
        scalars=1,
    )
    back, z1 = lax.optimization_barrier((back.reshape(32, 16, 256), z1))
    z2 = next_pair(z1)
    x2 = swap(z1, "xl")
    back = lax.all_to_all(back, LON_AXES, 0, 0)
    back, z2, x2 = lax.optimization_barrier((back, z2, x2))
    mixed = call(
        inverse_kernel,
        shape((16, 64, 128)),
        [pltpu.VMEM((32, 16, 256), F32)],
        "latitude_back",
        (back, tokens, normed, small),
    )
    mixed, z2 = lax.optimization_barrier((mixed.reshape(8, 2, 64, 128), z2))
    x3 = swap(z2, "xl")
    mixed = lax.all_to_all(mixed, OCT_AXES, 0, 0)
    mixed, x3 = lax.optimization_barrier((mixed, x3))
    own = call(
        second_norm_kernel,
        shape((C, 256)),
        [pltpu.VMEM((C, 256), F32)],
        "second_norm",
        (place, mixed, swap(mixed, "xh"), sums),
        scalars=1,
    )
    own_out, other_out = call(
        mlp_kernel,
        [shape((C, 256), F32), shape((C, 256))],
        [],
        "channel_mlp",
        (packed, z0, z1, z2, x0, x1, x2, x3, own, swap(own, "core")),
        limit=30 << 20,
    )
    keep, send = call(
        core_sum_kernel,
        [shape((512, 256), F32), shape((512, 256))],
        [],
        "core_sum",
        (place, own_out, swap(other_out, "core")),
        scalars=1,
    )
    result = call(
        finish_kernel, shape((8, 2, 64, 128)), [], "finish", (mixed, keep, swap(send, "xh"))
    )
    result = lax.all_to_all(lax.optimization_barrier(result), OCT_AXES, 0, 0)
    return result.reshape(16, 64, 128).transpose(2, 0, 1)


def solution(mesh):
    fine = Mesh(
        mesh.devices.reshape(2, 8, 2, 2, 2, 4), ("zl", "y", "core", "xh", "xl", "zh")
    )
    return jax.shard_map(
        per_device,
        mesh=fine,
        in_specs=(
            P(None, LON_AXES, CH_AXES),
            P(CH_AXES),
            P(None, CH_AXES, None),
            P(None, CH_AXES, None),
            P(CH_AXES),
            P(None, CH_AXES),
            P(CH_AXES, None),
        ),
        out_specs=P(None, LON_AXES, CH_AXES),
        check_vma=False,
    )
```

time: 177 us -> 161 us (0.910)
  the two profiles are of different devices: /device:TPU:32 before, /device:TPU:1 now
where the time goes in v2:
time: 161 us; the launch traced here: 159 us
  blocking collectives  64.5 us (40%)
  starting transfers between devices  49.9 us (31%)
  waiting for transfers between devices  29.8 us (19%)
  Pallas kernels  11.5 us (7%)
  local copies, waits for them, and re-layouts  2.04 us (1%)
    ppermute x9, starting transfers between devices, swap(): return lax.ppermute(values, axis, [(0, 1), (1, 0)])  30.7 us
    all_to_all x1, blocking collectives, per_device(): rows = lax.all_to_all(rows, LON_AXES, 0, 0)  21.8 us
    ppermute x9, waiting for transfers between devices, swap(): return lax.ppermute(values, axis, [(0, 1), (1, 0)])  17.2 us
    all_to_all x1, blocking collectives, per_device(): back = lax.all_to_all(back, LON_AXES, 0, 0)  16.8 us
    ppermute x2, starting transfers between devices, next_pair(): return lax.ppermute(values, ('zl', 'zh'), pairs)  15.3 us
    all_to_all x1, blocking collectives, per_device(): mixed = lax.all_to_all(mixed, OCT_AXES, 0, 0)  13.6 us
    all_to_all x1, blocking collectives, per_device(): result = lax.all_to_all(lax.optimization_barrier(result), OCT_AXES, 0, 0)  12.4 us
    ppermute x2, waiting for transfers between devices, next_pair(): return lax.ppermute(values, ('zl', 'zh'), pairs)  11.9 us
  transfers between devices with their start and end apart: 12, of which 6 were waited for; matrix products, arithmetic and copies ran while one was open for 0% of the time, Pallas kernels for 0%

profile of v2, /device:TPU:1, one launch (start us, length us, event | category | flops | bytes accessed | tf_op | source)
XLA Modules:
  0.0 158.8 jit_solution(12115680133523946114)
XLA Ops:
  0.6 2.9 %setup.1 = (bf16[2,128,1024]{2,1,0:T(8,128)(2,1)}, f32[16,40,128]{2,1,0:T(8,128)}) custom-call(s32[3]{0:T(128)} %pad_add_fusion.place_ref, bf16[1024,256]{1,0:T(8,128)(2,1)} %up_ref.1, bf16[256,1024]{1,0:T(8,128)(2,1)} %down_ref.1, bf16[16,64,128]{2,1,0:T(8,128)(2,1)} %bitcast.13, bf16[64]{0:T(256)(128)(2,1)} %gain_ref.1), custom_call_target="tpu_custom_call" | custom-call | tf_op jit(solution)/shard_map/setup/pallas_call | solution.py:144
  3.5 4.0 %collective-permute-start.1 = (bf16[2,128,1024]{2,1,0:T(8,128)(2,1)}, bf16[2,128,1024]{2,1,0:T(8,128)(2,1)S(1)}, u32[]{:S(2)}, u32[]{:S(2)}) collective-permute-start(bf16[2,128,1024]{2,1,0:T(8,128)(2,1)} %get-tuple-element.32.refs_0_), channel_id=1, source_target_pairs={{0,4},{4,0},{1,5},{5,1},{2,6},{6,2},{3,7},{7,3},{8,12},{12,8},{9,1... | collective-permute-start | bytes 1572872 | tf_op jit(solution)/shard_map/ppermute | solution.py:311
  7.5 10.7 %collective-permute-start = (bf16[2,128,1024]{2,1,0:T(8,128)(2,1)}, bf16[2,128,1024]{2,1,0:T(8,128)(2,1)S(1)}, u32[]{:S(2)}, u32[]{:S(2)}) collective-permute-start(bf16[2,128,1024]{2,1,0:T(8,128)(2,1)} %get-tuple-element.32.refs_0_), channel_id=1, source_target_pairs={{256,1},{0,259},{257,2},{1,256},{258,3},{2,257},{259,0},{3,258},{2... | collective-permute-start | bytes 1572872 | tf_op jit(solution)/shard_map/ppermute | solution.py:319
  18.2 4.0 %all-to-all-start = ((f32[16,40,128]{2,1,0:T(8,128)}), f32[16,40,128]{2,1,0:T(8,128)S(1)}, u32[]{:S(2)}, u32[]{:S(2)}) async-start(f32[16,40,128]{2,1,0:T(8,128)} %get-tuple-element.31), calls=%async_computation | async-start | bytes 655360 | tf_op jit(solution)/shard_map/all_to_all | solution.py:330
  23.1 11.9 %collective-permute-done.refs_1_ = bf16[2,128,1024]{2,1,0:T(8,128)(2,1)S(1)} collective-permute-done((bf16[2,128,1024]{2,1,0:T(8,128)(2,1)}, bf16[2,128,1024]{2,1,0:T(8,128)(2,1)S(1)}, u32[]{:S(2)}, u32[]{:S(2)}) %collective-permute-start) | collective-permute-done | bytes 524320 | tf_op jit(solution)/shard_map/ppermute | solution.py:319
  36.5 2.2 %collective-permute-start.3 = (bf16[2,128,1024]{2,1,0:T(8,128)(2,1)S(1)}, bf16[2,128,1024]{2,1,0:T(8,128)(2,1)S(1)}, u32[]{:S(2)}, u32[]{:S(2)}) collective-permute-start(bf16[2,128,1024]{2,1,0:T(8,128)(2,1)S(1)} %collective-permute-done.refs_1_), channel_id=1, source_target_pairs={{0,4},{4,0},{1,5},{5,1},{2,6},{6,2},{3,7},{7,3},{8,12},{12,8},{9,1... | collective-permute-start | bytes 1572872 | tf_op jit(solution)/shard_map/ppermute | solution.py:311
  38.6 5.0 %collective-permute-start.2 = (bf16[2,128,1024]{2,1,0:T(8,128)(2,1)S(1)}, bf16[2,128,1024]{2,1,0:T(8,128)(2,1)S(1)}, u32[]{:S(2)}, u32[]{:S(2)}) collective-permute-start(bf16[2,128,1024]{2,1,0:T(8,128)(2,1)S(1)} %collective-permute-done.refs_1_), channel_id=1, source_target_pairs={{0,256},{256,0},{1,257},{257,1},{2,258},{258,2},{3,259},{259,3},{4... | collective-permute-start | bytes 1572872 | tf_op jit(solution)/shard_map/ppermute | solution.py:311
  43.7 21.8 %all_to_all.25 = bf16[32,16,256]{2,1,0:T(8,128)(2,1)S(1)} all-to-all(bf16[32,16,256]{2,1,0:T(8,128)(2,1)S(1)} %get-tuple-element.37), channel_id=1, replica_groups=mesh['zl'=2,'y'=8,'core'=2,'xh'=2,'xl'=2,'zh'=4] {'zl','y','core'}, dimensions={0} | all-to-all | bytes 524288 | tf_op jit(solution)/shard_map/all_to_all | solution.py:354
  66.1 2.5 %spectral.1 = bf16[512,256]{1,0:T(8,128)(2,1)S(1)} custom-call(s32[3]{0:T(128)S(1)} %copy-done.4, bf16[512,256]{1,0:T(8,128)(2,1)S(1)} %bitcast.18, bf16[512,512]{1,0:T(8,128)(2,1)S(1)} %copy-done.3, bf16[512,512]{1,0:T(8,128)(2,1)S(1)} %copy-done.2, bf16[432,256]{1,0:T(8,128)(2,1)S(1)} %constant_dynamic-update-slice_fusion.small_ref), custom_call_target="tpu_custom_call" | custom-call | tf_op jit(solution)/shard_map/spectral/pallas_call | solution.py:295
  68.6 3.2 %collective-permute-start.5 = (bf16[2,128,1024]{2,1,0:T(8,128)(2,1)S(1)}, bf16[2,128,1024]{2,1,0:T(8,128)(2,1)S(1)}, u32[]{:S(2)}, u32[]{:S(2)}) collective-permute-start(bf16[2,128,1024]{2,1,0:T(8,128)(2,1)S(1)} %collective-permute-done.2.refs_2_), channel_id=1, source_target_pairs={{0,4},{4,0},{1,5},{5,1},{2,6},{6,2},{3,7},{7,3},{8,12},{12,8},{9,1... | collective-permute-start | bytes 1572872 | tf_op jit(solution)/shard_map/ppermute | solution.py:311
  71.8 4.6 %collective-permute-start.4 = (bf16[2,128,1024]{2,1,0:T(8,128)(2,1)S(1)}, bf16[2,128,1024]{2,1,0:T(8,128)(2,1)S(1)}, u32[]{:S(2)}, u32[]{:S(2)}) collective-permute-start(bf16[2,128,1024]{2,1,0:T(8,128)(2,1)S(1)} %collective-permute-done.2.refs_2_), channel_id=1, source_target_pairs={{256,1},{0,259},{257,2},{1,256},{258,3},{2,257},{259,0},{3,258},{2... | collective-permute-start | bytes 1572872 | tf_op jit(solution)/shard_map/ppermute | solution.py:319
  76.4 16.8 %all_to_all.26.rows_ref = bf16[32,16,256]{2,1,0:T(8,128)(2,1)S(1)} all-to-all(bf16[32,16,256]{2,1,0:T(8,128)(2,1)S(1)} %bitcast.17), channel_id=1, replica_groups=mesh['zl'=2,'y'=8,'core'=2,'xh'=2,'xl'=2,'zh'=4] {'zl','y','core'}, dimensions={0} | all-to-all | bytes 524288 | tf_op jit(solution)/shard_map/all_to_all | solution.py:373
  93.8 2.0 %collective-permute-start.6 = (bf16[2,128,1024]{2,1,0:T(8,128)(2,1)S(1)}, bf16[2,128,1024]{2,1,0:T(8,128)(2,1)S(1)}, u32[]{:S(2)}, u32[]{:S(2)}) collective-permute-start(bf16[2,128,1024]{2,1,0:T(8,128)(2,1)S(1)} %collective-permute-done.4.refs_3_), channel_id=1, source_target_pairs={{0,4},{4,0},{1,5},{5,1},{2,6},{6,2},{3,7},{7,3},{8,12},{12,8},{9,1... | collective-permute-start | bytes 1572872 | tf_op jit(solution)/shard_map/ppermute | solution.py:311
  95.8 13.6 %all_to_all.27.own_ref.mixed_ref = bf16[8,2,64,128]{3,2,1,0:T(8,128)(2,1)S(1)} all-to-all(bf16[8,2,64,128]{3,2,1,0:T(8,128)(2,1)S(1)} %bitcast.16), channel_id=1, replica_groups=mesh['zl'=2,'y'=8,'core'=2,'xh'=2,'xl'=2,'zh'=4] {'xl','zh'}, dimensions={0} | all-to-all | bytes 524288 | tf_op jit(solution)/shard_map/all_to_all | solution.py:384
  109.3 2.8 %collective-permute-start.7 = (bf16[8,2,64,128]{3,2,1,0:T(8,128)(2,1)S(1)}, bf16[8,2,64,128]{3,2,1,0:T(8,128)(2,1)S(1)}, u32[]{:S(2)}, u32[]{:S(2)}) collective-permute-start(bf16[8,2,64,128]{3,2,1,0:T(8,128)(2,1)S(1)} %all_to_all.27.own_ref.mixed_ref), channel_id=1, source_target_pairs={{0,8},{8,0},{1,9},{9,1},{2,10},{10,2},{3,11},{11,3},{4,12},{12,4},... | collective-permute-start | bytes 786440 | tf_op jit(solution)/shard_map/ppermute | solution.py:311
  112.1 5.9 %collective-permute-done.7.other_ref = bf16[8,2,64,128]{3,2,1,0:T(8,128)(2,1)S(1)} collective-permute-done((bf16[8,2,64,128]{3,2,1,0:T(8,128)(2,1)S(1)}, bf16[8,2,64,128]{3,2,1,0:T(8,128)(2,1)S(1)}, u32[]{:S(2)}, u32[]{:S(2)}) %collective-permute-start.7) | collective-permute-done | bytes 262176 | tf_op jit(solution)/shard_map/ppermute | solution.py:311
  119.0 6.5 %collective-permute-start.8 = (bf16[1024,256]{1,0:T(8,128)(2,1)S(1)}, bf16[1024,256]{1,0:T(8,128)(2,1)S(1)}, u32[]{:S(2)}, u32[]{:S(2)}) collective-permute-start(bf16[1024,256]{1,0:T(8,128)(2,1)S(1)} %second_norm.1.refs_8_), channel_id=1, source_target_pairs={{0,16},{16,0},{1,17},{17,1},{2,18},{18,2},{3,19},{19,3},{4,20},{20... | collective-permute-start | bytes 1572872 | tf_op jit(solution)/shard_map/ppermute | solution.py:311
  125.6 1.5 collective-permute-done.8.refs_9_
  127.1 3.1 %channel_mlp.1 = (f32[1024,256]{1,0:T(8,128)S(1)}, bf16[1024,256]{1,0:T(8,128)(2,1)S(1)}) custom-call(bf16[2,128,1024]{2,1,0:T(8,128)(2,1)S(1)} %copy-done.1, bf16[2,128,1024]{2,1,0:T(8,128)(2,1)S(1)} %collective-permute-done.refs_1_, bf16[2,128,1024]{2,1,0:T(8,128)(2,1)S(1)} %collective-permute-done.2.refs_2_, ...), custom_call_target="tpu_custom_call" | custom-call | tf_op jit(solution)/shard_map/channel_mlp/pallas_call | solution.py:295
  130.2 2.3 %collective-permute-start.9 = (bf16[1024,256]{1,0:T(8,128)(2,1)S(1)}, bf16[1024,256]{1,0:T(8,128)(2,1)S(1)}, u32[]{:S(2)}, u32[]{:S(2)}) collective-permute-start(bf16[1024,256]{1,0:T(8,128)(2,1)S(1)} %get-tuple-element.54), channel_id=1, source_target_pairs={{0,16},{16,0},{1,17},{17,1},{2,18},{18,2},{3,19},{19,3},{4,20},{20... | collective-permute-start | bytes 1572872 | tf_op jit(solution)/shard_map/ppermute | solution.py:311
  132.5 1.5 collective-permute-done.9.other_ref
  134.7 2.7 %collective-permute-start.10 = (bf16[512,256]{1,0:T(8,128)(2,1)S(1)}, bf16[512,256]{1,0:T(8,128)(2,1)S(1)}, u32[]{:S(2)}, u32[]{:S(2)}) collective-permute-start(bf16[512,256]{1,0:T(8,128)(2,1)S(1)} %get-tuple-element.56), channel_id=1, source_target_pairs={{0,8},{8,0},{1,9},{9,1},{2,10},{10,2},{3,11},{11,3},{4,12},{12,4},... | collective-permute-start | bytes 786440 | tf_op jit(solution)/shard_map/ppermute | solution.py:311
  137.3 8.2 %collective-permute-done.10.other_ref = bf16[512,256]{1,0:T(8,128)(2,1)S(1)} collective-permute-done((bf16[512,256]{1,0:T(8,128)(2,1)S(1)}, bf16[512,256]{1,0:T(8,128)(2,1)S(1)}, u32[]{:S(2)}, u32[]{:S(2)}) %collective-permute-start.10) | collective-permute-done | bytes 262176 | tf_op jit(solution)/shard_map/ppermute | solution.py:311
  145.7 12.4 %all_to_all.28 = bf16[8,2,64,128]{3,2,1,0:T(8,128)(2,1)S(1)} all-to-all(bf16[8,2,64,128]{3,2,1,0:T(8,128)(2,1)S(1)} %finish.1), channel_id=1, replica_groups=mesh['zl'=2,'y'=8,'core'=2,'xh'=2,'xl'=2,'zh'=4] {'xl','zh'}, dimensions={0} | all-to-all | bytes 524288 | tf_op jit(solution)/shard_map/all_to_all | solution.py:413
  (45 shorter events, 6.3 us)
Async XLA Ops:
  3.5 19.5 %collective-permute-start.1 = (bf16[2,128,1024]{2,1,0:T(8,128)(2,1)}, bf16[2,128,1024]{2,1,0:T(8,128)(2,1)S(1)}, u32[]{:S(2)}, u32[]{:S(2)}) collective-permute-start(bf16[2,128,1024]{2,1,0:T(8,128)(2,1)} %get-tuple-element.32.refs_0_), channel_id=1, source_target_pairs={{0,4},{4,0},{1,5},{5,1},{2,6},{6,2},{3,7},{7,3},{8,12},{12,8},{9,1... | collective-permute-start | bytes 1572872 | tf_op jit(solution)/shard_map/ppermute | solution.py:311
  7.5 27.5 %collective-permute-start = (bf16[2,128,1024]{2,1,0:T(8,128)(2,1)}, bf16[2,128,1024]{2,1,0:T(8,128)(2,1)S(1)}, u32[]{:S(2)}, u32[]{:S(2)}) collective-permute-start(bf16[2,128,1024]{2,1,0:T(8,128)(2,1)} %get-tuple-element.32.refs_0_), channel_id=1, source_target_pairs={{256,1},{0,259},{257,2},{1,256},{258,3},{2,257},{259,0},{3,258},{2... | collective-permute-start | bytes 1572872 | tf_op jit(solution)/shard_map/ppermute | solution.py:319
  18.2 4.1 %copy-start.7 = (bf16[64,256]{1,0:T(8,128)(2,1)S(1)}, bf16[64,256]{1,0:T(8,128)(2,1)}, u32[]{:S(2)}) copy-start(bf16[64,256]{1,0:T(8,128)(2,1)} %constant.35.clone) | copy-start | bytes 98308
  18.2 4.1 %copy-start.10 = (bf16[32,256]{1,0:T(8,128)(2,1)S(1)}, bf16[32,256]{1,0:T(8,128)(2,1)}, u32[]{:S(2)}) copy-start(bf16[32,256]{1,0:T(8,128)(2,1)} %constant.36.clone) | copy-start | bytes 49156
  18.2 4.1 %copy-start.9 = (bf16[32,256]{1,0:T(8,128)(2,1)S(1)}, bf16[32,256]{1,0:T(8,128)(2,1)}, u32[]{:S(2)}) copy-start(bf16[32,256]{1,0:T(8,128)(2,1)} %constant.37.clone) | copy-start | bytes 49156
  18.2 4.1 %copy-start.8 = (bf16[32,256]{1,0:T(8,128)(2,1)S(1)}, bf16[32,256]{1,0:T(8,128)(2,1)}, u32[]{:S(2)}) copy-start(bf16[32,256]{1,0:T(8,128)(2,1)} %constant.38.clone) | copy-start | bytes 49156
  18.2 4.1 %copy-start.5 = (bf16[2,64,64]{2,1,0:T(8,128)(2,1)S(1)}, bf16[2,64,64]{2,1,0:T(8,128)(2,1)}, u32[]{:S(2)}) copy-start(bf16[2,64,64]{2,1,0:T(8,128)(2,1)} %param.15) | copy-start | bytes 49156
  18.2 4.1 %copy-start.6 = (bf16[2,64,64]{2,1,0:T(8,128)(2,1)S(1)}, bf16[2,64,64]{2,1,0:T(8,128)(2,1)}, u32[]{:S(2)}) copy-start(bf16[2,64,64]{2,1,0:T(8,128)(2,1)} %param.16) | copy-start | bytes 49156
  18.2 17.4 %all-to-all-start = ((f32[16,40,128]{2,1,0:T(8,128)}), f32[16,40,128]{2,1,0:T(8,128)S(1)}, u32[]{:S(2)}, u32[]{:S(2)}) async-start(f32[16,40,128]{2,1,0:T(8,128)} %get-tuple-element.31), calls=%async_computation | async-start | bytes 655360 | tf_op jit(solution)/shard_map/all_to_all | solution.py:330
  22.2 13.4 %copy-start = (bf16[128,16,64]{0,2,1:T(8,128)(2,1)S(1)}, bf16[128,16,64]{0,2,1:T(8,128)(2,1)}, u32[]{:S(2)}) copy-start(bf16[128,16,64]{0,2,1:T(8,128)(2,1)} %param.13) | copy-start | bytes 786436
  22.4 0.7 copy-start.11
  23.1 42.4 %copy-start.2 = (bf16[512,512]{1,0:T(8,128)(2,1)S(1)}, bf16[512,512]{1,0:T(8,128)(2,1)}, u32[]{:S(2)}) copy-start(bf16[512,512]{1,0:T(8,128)(2,1)} %constant.40.clone.inverse_ref) | copy-start | bytes 1572868
  23.1 42.4 %copy-start.3 = (bf16[512,512]{1,0:T(8,128)(2,1)S(1)}, bf16[512,512]{1,0:T(8,128)(2,1)}, u32[]{:S(2)}) copy-start(bf16[512,512]{1,0:T(8,128)(2,1)} %constant.39.clone.lon_ref) | copy-start | bytes 1572868
  36.5 29.0 %collective-permute-start.3 = (bf16[2,128,1024]{2,1,0:T(8,128)(2,1)S(1)}, bf16[2,128,1024]{2,1,0:T(8,128)(2,1)S(1)}, u32[]{:S(2)}, u32[]{:S(2)}) collective-permute-start(bf16[2,128,1024]{2,1,0:T(8,128)(2,1)S(1)} %collective-permute-done.refs_1_), channel_id=1, source_target_pairs={{0,4},{4,0},{1,5},{5,1},{2,6},{6,2},{3,7},{7,3},{8,12},{12,8},{9,1... | collective-permute-start | bytes 1572872 | tf_op jit(solution)/shard_map/ppermute | solution.py:311
  38.6 26.8 %collective-permute-start.2 = (bf16[2,128,1024]{2,1,0:T(8,128)(2,1)S(1)}, bf16[2,128,1024]{2,1,0:T(8,128)(2,1)S(1)}, u32[]{:S(2)}, u32[]{:S(2)}) collective-permute-start(bf16[2,128,1024]{2,1,0:T(8,128)(2,1)S(1)} %collective-permute-done.refs_1_), channel_id=1, source_target_pairs={{0,256},{256,0},{1,257},{257,1},{2,258},{258,2},{3,259},{259,3},{4... | collective-permute-start | bytes 1572872 | tf_op jit(solution)/shard_map/ppermute | solution.py:311
  65.5 0.6 copy-start.4
  68.6 24.7 %collective-permute-start.5 = (bf16[2,128,1024]{2,1,0:T(8,128)(2,1)S(1)}, bf16[2,128,1024]{2,1,0:T(8,128)(2,1)S(1)}, u32[]{:S(2)}, u32[]{:S(2)}) collective-permute-start(bf16[2,128,1024]{2,1,0:T(8,128)(2,1)S(1)} %collective-permute-done.2.refs_2_), channel_id=1, source_target_pairs={{0,4},{4,0},{1,5},{5,1},{2,6},{6,2},{3,7},{7,3},{8,12},{12,8},{9,1... | collective-permute-start | bytes 1572872 | tf_op jit(solution)/shard_map/ppermute | solution.py:311
  71.8 21.4 %collective-permute-start.4 = (bf16[2,128,1024]{2,1,0:T(8,128)(2,1)S(1)}, bf16[2,128,1024]{2,1,0:T(8,128)(2,1)S(1)}, u32[]{:S(2)}, u32[]{:S(2)}) collective-permute-start(bf16[2,128,1024]{2,1,0:T(8,128)(2,1)S(1)} %collective-permute-done.2.refs_2_), channel_id=1, source_target_pairs={{256,1},{0,259},{257,2},{1,256},{258,3},{2,257},{259,0},{3,258},{2... | collective-permute-start | bytes 1572872 | tf_op jit(solution)/shard_map/ppermute | solution.py:319
  93.8 15.6 %collective-permute-start.6 = (bf16[2,128,1024]{2,1,0:T(8,128)(2,1)S(1)}, bf16[2,128,1024]{2,1,0:T(8,128)(2,1)S(1)}, u32[]{:S(2)}, u32[]{:S(2)}) collective-permute-start(bf16[2,128,1024]{2,1,0:T(8,128)(2,1)S(1)} %collective-permute-done.4.refs_3_), channel_id=1, source_target_pairs={{0,4},{4,0},{1,5},{5,1},{2,6},{6,2},{3,7},{7,3},{8,12},{12,8},{9,1... | collective-permute-start | bytes 1572872 | tf_op jit(solution)/shard_map/ppermute | solution.py:311
  109.3 17.7 %copy-start.1 = (bf16[2,128,1024]{2,1,0:T(8,128)(2,1)S(1)}, bf16[2,128,1024]{2,1,0:T(8,128)(2,1)}, u32[]{:S(2)}) copy-start(bf16[2,128,1024]{2,1,0:T(8,128)(2,1)} %get-tuple-element.32.refs_0_) | copy-start | bytes 1572868
  109.3 8.7 %collective-permute-start.7 = (bf16[8,2,64,128]{3,2,1,0:T(8,128)(2,1)S(1)}, bf16[8,2,64,128]{3,2,1,0:T(8,128)(2,1)S(1)}, u32[]{:S(2)}, u32[]{:S(2)}) collective-permute-start(bf16[8,2,64,128]{3,2,1,0:T(8,128)(2,1)S(1)} %all_to_all.27.own_ref.mixed_ref), channel_id=1, source_target_pairs={{0,8},{8,0},{1,9},{9,1},{2,10},{10,2},{3,11},{11,3},{4,12},{12,4},... | collective-permute-start | bytes 786440 | tf_op jit(solution)/shard_map/ppermute | solution.py:311
  119.0 8.0 %collective-permute-start.8 = (bf16[1024,256]{1,0:T(8,128)(2,1)S(1)}, bf16[1024,256]{1,0:T(8,128)(2,1)S(1)}, u32[]{:S(2)}, u32[]{:S(2)}) collective-permute-start(bf16[1024,256]{1,0:T(8,128)(2,1)S(1)} %second_norm.1.refs_8_), channel_id=1, source_target_pairs={{0,16},{16,0},{1,17},{17,1},{2,18},{18,2},{3,19},{19,3},{4,20},{20... | collective-permute-start | bytes 1572872 | tf_op jit(solution)/shard_map/ppermute | solution.py:311
  130.2 3.8 %collective-permute-start.9 = (bf16[1024,256]{1,0:T(8,128)(2,1)S(1)}, bf16[1024,256]{1,0:T(8,128)(2,1)S(1)}, u32[]{:S(2)}, u32[]{:S(2)}) collective-permute-start(bf16[1024,256]{1,0:T(8,128)(2,1)S(1)} %get-tuple-element.54), channel_id=1, source_target_pairs={{0,16},{16,0},{1,17},{17,1},{2,18},{18,2},{3,19},{19,3},{4,20},{20... | collective-permute-start | bytes 1572872 | tf_op jit(solution)/shard_map/ppermute | solution.py:311
  134.7 10.9 %collective-permute-start.10 = (bf16[512,256]{1,0:T(8,128)(2,1)S(1)}, bf16[512,256]{1,0:T(8,128)(2,1)S(1)}, u32[]{:S(2)}, u32[]{:S(2)}) collective-permute-start(bf16[512,256]{1,0:T(8,128)(2,1)S(1)} %get-tuple-element.56), channel_id=1, source_target_pairs={{0,8},{8,0},{1,9},{9,1},{2,10},{10,2},{3,11},{11,3},{4,12},{12,4},... | collective-permute-start | bytes 786440 | tf_op jit(solution)/shard_map/ppermute | solution.py:311

commit v3 on v2

--- a/solution.py
+++ b/solution.py
@@ -23,7 +23,6 @@
 
 LON_AXES = ("zl", "y", "core")
 CH_AXES = ("xh", "xl", "zh")
-OCT_AXES = ("xl", "zh")
 NT = (((1,), (1,)), ((), ()))
 TN = (((0,), (0,)), ((), ()))
 
@@ -109,8 +108,8 @@
     return jnp.sum(jnp.where(diagonal, row, 0.0), axis=1, keepdims=True)
 
 
-def setup_kernel(place_ref, up_ref, down_ref, tokens_ref, gain_ref, packed_ref, sums_ref, up_part, tokens_part, gain_part, sems):
-    half = pl.ds(pl.multiple_of(place_ref[0] * 128, 128), 128)
+def setup_kernel(up_ref, down_ref, tokens_ref, gain_ref, packed_ref, sums_ref, up_part, tokens_part, gain_part, sems):
+    half = pl.ds(pl.multiple_of(lax.axis_index("core") * 128, 128), 128)
     pairs = [
         (tokens_ref, tokens_part),
         (gain_ref, gain_part),
@@ -144,7 +143,7 @@
     return pl.pallas_call(
         setup_kernel,
         out_shape=[shape((2, 128, C)), shape((16, 40, 128), F32)],
-        in_specs=[pl.BlockSpec(memory_space=pltpu.SMEM)] + [pl.BlockSpec(memory_space=pl.ANY)] * 4,
+        in_specs=[pl.BlockSpec(memory_space=pl.ANY)] * 4,
         out_specs=[VMEM] * 2,
         scratch_shapes=[
             pltpu.VMEM((C, 128), BF16),
@@ -178,8 +177,9 @@
     out_ref[...] = wide[...].astype(BF16)
 
 
-def spectral_kernel(place_ref, rows_ref, lon_ref, inverse_ref, small_ref, out_ref, modes):
+def spectral_kernel(rows_ref, lon_ref, inverse_ref, small_ref, out_ref, modes):
     waves = jnp.dot(lon_ref[...], rows_ref[...], preferred_element_type=F32).astype(BF16)
+    at_edge = lax.axis_index("zl") + lax.axis_index("y") + lax.axis_index("core") == 0
     row = lax.broadcasted_iota(jnp.int32, (256, 8), 0) // 64
     spot = lax.broadcasted_iota(jnp.int32, (256, 8), 1)
     blocks = jnp.where(row == spot, 1.0, 0.0).astype(BF16)
@@ -202,7 +202,7 @@
             ]
             found.append(tiles[0] * mask[0] + tiles[1] * mask[1])
         plain, edge = found
-        return [jnp.where(place_ref[1] == 1, edge, plain).astype(BF16), plain.astype(BF16)]
+        return [jnp.where(at_edge, edge, plain).astype(BF16), plain.astype(BF16)]
 
     def rows_of(start, count):
         return small_ref[start : start + count]
@@ -235,30 +235,27 @@
         both = lax.dot_general(rows, table, TN, preferred_element_type=F32)
         filtered = (both[:64, :LAT] + both[64:, LAT:]).astype(BF16).astype(F32)
         mixed = tokens_ref[w].astype(F32) + normed_ref[w].astype(F32) + filtered
-        mixed_ref[w] = mixed.astype(BF16)
-
-
-def second_norm_kernel(place_ref, own_ref, other_ref, sums_ref, out_ref, both):
-    xh = place_ref[2]
+        mixed_ref[0, w // 2, w % 2] = mixed.astype(BF16)
+        mixed_ref[1, w // 2, w % 2] = mixed.astype(BF16)
+
+
+def second_norm_kernel(mixed_ref, sums_ref, out_ref):
     for w in range(2):
-        for d in range(8):
-            mine = pl.ds(pl.multiple_of(xh * 512 + d * 64, 64), 64)
-            theirs = pl.ds(pl.multiple_of((1 - xh) * 512 + d * 64, 64), 64)
-            both[mine, w * 128 : w * 128 + 128] = own_ref[d, w].astype(F32)
-            both[theirs, w * 128 : w * 128 + 128] = other_ref[d, w].astype(F32)
-    wide = both[...]
-    mean = jnp.sum(wide, axis=0, keepdims=True) / C
-    power = jnp.sum(wide * wide, axis=0, keepdims=True) / C - mean * mean
-    scale = lax.rsqrt(power + EPSILON)
-    for block in range(16):
-        rows = slice(block * 64, block * 64 + 64)
-        gain = column_of(sums_ref[block, 32:33, :64])
-        out_ref[rows] = ((both[rows] - mean) * scale * gain).astype(BF16)
+        wide = mixed_ref[:, w].astype(F32).reshape(C, 128)
+        mean = jnp.sum(wide, axis=0, keepdims=True) / C
+        power = jnp.sum(wide * wide, axis=0, keepdims=True) / C - mean * mean
+        scale = lax.rsqrt(power + EPSILON)
+        for block in range(16):
+            rows = slice(block * 64, block * 64 + 64)
+            gain = column_of(sums_ref[block, 32:33, :64])
+            values = mixed_ref[block, w].astype(F32)
+            out = (values - mean) * scale * gain
+            out_ref[rows, w * 128 : w * 128 + 128] = out.astype(BF16)
 
 
 def mlp_kernel(*refs):
-    pieces = refs[:8]
-    own_ref, other_ref, own_out, other_out = refs[8:]
+    p0, z0, z1, z2, x0, x12, x3, own_ref, other_ref, own_out, other_out = refs
+    pieces = [p0, z0, z1, z2, x0, x12.at[0], x12.at[1], x3]
     group = jnp.concatenate([own_ref[...], other_ref[...]], axis=1)
     total = None
     for first, second in zip(pieces[0::2], pieces[1::2]):
@@ -272,25 +269,26 @@
     other_out[...] = total[:, 256:].astype(BF16)
 
 
-def core_sum_kernel(place_ref, own_ref, other_ref, keep_ref, send_ref):
-    xh = place_ref[2]
+def core_sum_kernel(own_ref, other_ref, keep_ref, send_ref):
+    xh = lax.axis_index("xh")
     mine = pl.ds(pl.multiple_of(xh * 512, 512), 512)
     theirs = pl.ds(pl.multiple_of((1 - xh) * 512, 512), 512)
     keep_ref[...] = own_ref[mine] + other_ref[mine].astype(F32)
     send_ref[...] = (own_ref[theirs] + other_ref[theirs].astype(F32)).astype(BF16)
 
 
-def finish_kernel(mixed_ref, keep_ref, other_ref, out_ref):
+def finish_kernel(wide_ref, keep_ref, other_ref, out_ref):
+    xh = lax.axis_index("xh")
     for d in range(8):
         rows = slice(d * 64, d * 64 + 64)
         branch = keep_ref[rows] + other_ref[rows].astype(F32)
         for w in range(2):
-            sums = mixed_ref[d, w].astype(F32) + branch[:, w * 128 : w * 128 + 128]
+            sums = wide_ref[xh * 8 + d, w].astype(F32) + branch[:, w * 128 : w * 128 + 128]
             out_ref[d, w] = sums.astype(BF16)
 
 
-def call(kernel, shapes, scratch, name, args, scalars=0, limit=10 << 20):
-    specs = [pl.BlockSpec(memory_space=pltpu.SMEM)] * scalars + [VMEM] * (len(args) - scalars)
+def call(kernel, shapes, scratch, name, args, limit=10 << 20):
+    specs = [VMEM] * len(args)
     many = isinstance(shapes, list)
     return pl.pallas_call(
         kernel,
@@ -320,11 +318,8 @@
 
 
 def per_device(grid_state, first_gain, spectral_first, spectral_second, second_gain, up_weight, down_weight):
-    zl, core = lax.axis_index("zl"), lax.axis_index("core")
-    edge = (zl + lax.axis_index("y") + core) == 0
-    place = jnp.stack([core, edge.astype(jnp.int32), lax.axis_index("xh")])
     tokens = grid_state.transpose(1, 2, 0)
-    packed, sums = setup(place, up_weight, down_weight, tokens, second_gain)
+    packed, sums = setup(up_weight, down_weight, tokens, second_gain)
     z0 = next_pair(packed)
     x0 = swap(packed, "xl")
     sums = lax.all_to_all(sums, CH_AXES, 0, 0)
@@ -350,53 +345,43 @@
     )
     rows, z0 = lax.optimization_barrier((rows, z0))
     z1 = swap(z0, "zl")
-    x1 = swap(z0, "xl")
     rows = lax.all_to_all(rows, LON_AXES, 0, 0)
-    rows, z1, x1 = lax.optimization_barrier((rows, z1, x1))
+    rows, z1 = lax.optimization_barrier((rows, z1))
+    x12 = swap(jnp.stack([z0, z1]), "xl")
     back = call(
         spectral_kernel,
         shape((LON, 256)),
         [pltpu.VMEM((LON, 256), BF16)],
         "spectral",
         (
-            place,
             rows.reshape(LON, 256),
             jnp.asarray(lon_table(), BF16),
             jnp.asarray(lon_inverse_table(), BF16),
             small,
         ),
-        scalars=1,
     )
     back, z1 = lax.optimization_barrier((back.reshape(32, 16, 256), z1))
     z2 = next_pair(z1)
-    x2 = swap(z1, "xl")
     back = lax.all_to_all(back, LON_AXES, 0, 0)
-    back, z2, x2 = lax.optimization_barrier((back, z2, x2))
+    back, z2, x12 = lax.optimization_barrier((back, z2, x12))
     mixed = call(
         inverse_kernel,
-        shape((16, 64, 128)),
+        shape((2, 8, 2, 64, 128)),
         [pltpu.VMEM((32, 16, 256), F32)],
         "latitude_back",
         (back, tokens, normed, small),
     )
-    mixed, z2 = lax.optimization_barrier((mixed.reshape(8, 2, 64, 128), z2))
+    mixed, z2 = lax.optimization_barrier((mixed, z2))
     x3 = swap(z2, "xl")
-    mixed = lax.all_to_all(mixed, OCT_AXES, 0, 0)
-    mixed, x3 = lax.optimization_barrier((mixed, x3))
-    own = call(
-        second_norm_kernel,
-        shape((C, 256)),
-        [pltpu.VMEM((C, 256), F32)],
-        "second_norm",
-        (place, mixed, swap(mixed, "xh"), sums),
-        scalars=1,
-    )
+    wide = lax.all_to_all(mixed.reshape(16, 2, 64, 128), CH_AXES, 0, 0)
+    wide = lax.optimization_barrier(wide)
+    own = call(second_norm_kernel, shape((C, 256)), [], "second_norm", (wide, sums))
     own_out, other_out = call(
         mlp_kernel,
         [shape((C, 256), F32), shape((C, 256))],
         [],
         "channel_mlp",
-        (packed, z0, z1, z2, x0, x1, x2, x3, own, swap(own, "core")),
+        (packed, z0, z1, z2, x0, x12, x3, own, swap(own, "core")),
         limit=30 << 20,
     )
     keep, send = call(
@@ -404,13 +389,10 @@
         [shape((512, 256), F32), shape((512, 256))],
         [],
         "core_sum",
-        (place, own_out, swap(other_out, "core")),
-        scalars=1,
-    )
-    result = call(
-        finish_kernel, shape((8, 2, 64, 128)), [], "finish", (mixed, keep, swap(send, "xh"))
-    )
-    result = lax.all_to_all(lax.optimization_barrier(result), OCT_AXES, 0, 0)
+        (own_out, swap(other_out, "core")),
+    )
+    result = call(finish_kernel, shape((8, 2, 64, 128)), [], "finish", (wide, keep, swap(send, "xh")))
+    result = lax.all_to_all(lax.optimization_barrier(result), ("xl", "zh"), 0, 0)
     return result.reshape(16, 64, 128).transpose(2, 0, 1)
 
 

time: 161 us -> 153 us (0.950)
  blocking collectives: 64.5 us -> 51.6 us
  waiting for transfers between devices: 29.8 us -> 37.5 us
    all_to_all x0 -> x1, waiting for transfers between devices: none -> 13.7 us  [per_device(): wide = lax.all_to_all(mixed.reshape(16, 2, 64, 128), CH_AXES, 0, 0)]
    all_to_all x2 -> x1, blocking collectives: 26 us -> 13.3 us  [per_device(): lax.all_to_all(lax.optimization_barrier(result), ('xl', 'zh'), 0, 0)]
    ppermute x9 -> x7, starting transfers between devices: 30.7 us -> 23.8 us  [swap(): return lax.ppermute(values, axis, [(0, 1), (1, 0)])]
    ppermute x9 -> x7, waiting for transfers between devices: 17.2 us -> 11.3 us  [swap(): return lax.ppermute(values, axis, [(0, 1), (1, 0)])]
    all_to_all x0 -> x1, starting transfers between devices: none -> 5.31 us  [per_device(): wide = lax.all_to_all(mixed.reshape(16, 2, 64, 128), CH_AXES, 0, 0)]
  transfers between devices with their start and end apart: 12 -> 11, of which waited for: 6 -> 6; matrix products, arithmetic and copies ran while one was open for 0% -> 0% of each run, Pallas kernels for 0% -> 2%
where the time goes in v3:
time: 153 us; the launch traced here: 151 us
  blocking collectives  51.6 us (34%)
  starting transfers between devices  48.4 us (32%)
  waiting for transfers between devices  37.5 us (25%)
  Pallas kernels  11.3 us (7%)
    ppermute x7, starting transfers between devices, swap(): return lax.ppermute(values, axis, [(0, 1), (1, 0)])  23.8 us
    all_to_all x1, blocking collectives, per_device(): rows = lax.all_to_all(rows, LON_AXES, 0, 0)  21.5 us
    all_to_all x1, blocking collectives, per_device(): back = lax.all_to_all(back, LON_AXES, 0, 0)  16.8 us
    ppermute x2, starting transfers between devices, next_pair(): return lax.ppermute(values, ('zl', 'zh'), pairs)  15.3 us
    all_to_all x1, waiting for transfers between devices, per_device(): wide = lax.all_to_all(mixed.reshape(16, 2, 64, 128), CH_AXES, 0, 0)  13.7 us
    all_to_all x1, blocking collectives, per_device(): lax.all_to_all(lax.optimization_barrier(result), ('xl', 'zh'), 0, 0)  13.3 us
    ppermute x2, waiting for transfers between devices, next_pair(): return lax.ppermute(values, ('zl', 'zh'), pairs)  11.9 us
    ppermute x7, waiting for transfers between devices, swap(): return lax.ppermute(values, axis, [(0, 1), (1, 0)])  11.3 us
  transfers between devices with their start and end apart: 11, of which 6 were waited for; matrix products, arithmetic and copies ran while one was open for 0% of the time, Pallas kernels for 2%

profile of v3, /device:TPU:1, one launch (start us, length us, event | category | flops | bytes accessed | tf_op | source)
XLA Modules:
  0.0 150.7 jit_solution(12691489562342662407)
XLA Ops:
  0.0 2.3 %setup.1 = (bf16[2,128,1024]{2,1,0:T(8,128)(2,1)}, f32[16,40,128]{2,1,0:T(8,128)}) custom-call(bf16[1024,256]{1,0:T(8,128)(2,1)} %up_ref.1, bf16[256,1024]{1,0:T(8,128)(2,1)} %down_ref.1, bf16[16,64,128]{2,1,0:T(8,128)(2,1)} %bitcast.12, bf16[64]{0:T(256)(128)(2,1)} %gain_ref.1), custom_call_target="tpu_custom_call" | custom-call | tf_op jit(solution)/shard_map/setup/pallas_call | solution.py:143
  2.3 4.0 %collective-permute-start.1 = (bf16[2,128,1024]{2,1,0:T(8,128)(2,1)}, bf16[2,128,1024]{2,1,0:T(8,128)(2,1)S(1)}, u32[]{:S(2)}, u32[]{:S(2)}) collective-permute-start(bf16[2,128,1024]{2,1,0:T(8,128)(2,1)} %get-tuple-element.29.refs_0_), channel_id=1, source_target_pairs={{0,4},{4,0},{1,5},{5,1},{2,6},{6,2},{3,7},{7,3},{8,12},{12,8},{9,1... | collective-permute-start | bytes 1572872 | tf_op jit(solution)/shard_map/ppermute | solution.py:309
  6.2 10.7 %collective-permute-start = (bf16[2,128,1024]{2,1,0:T(8,128)(2,1)}, bf16[2,128,1024]{2,1,0:T(8,128)(2,1)S(1)}, u32[]{:S(2)}, u32[]{:S(2)}) collective-permute-start(bf16[2,128,1024]{2,1,0:T(8,128)(2,1)} %get-tuple-element.29.refs_0_), channel_id=1, source_target_pairs={{256,1},{0,259},{257,2},{1,256},{258,3},{2,257},{259,0},{3,258},{2... | collective-permute-start | bytes 1572872 | tf_op jit(solution)/shard_map/ppermute | solution.py:317
  17.0 4.0 %all-to-all-start = ((f32[16,40,128]{2,1,0:T(8,128)}), f32[16,40,128]{2,1,0:T(8,128)S(1)}, u32[]{:S(2)}, u32[]{:S(2)}) async-start(f32[16,40,128]{2,1,0:T(8,128)} %get-tuple-element.28), calls=%async_computation | async-start | bytes 655360 | tf_op jit(solution)/shard_map/all_to_all | solution.py:325
  21.8 11.9 %collective-permute-done.refs_1_ = bf16[2,128,1024]{2,1,0:T(8,128)(2,1)S(1)} collective-permute-done((bf16[2,128,1024]{2,1,0:T(8,128)(2,1)}, bf16[2,128,1024]{2,1,0:T(8,128)(2,1)S(1)}, u32[]{:S(2)}, u32[]{:S(2)}) %collective-permute-start) | collective-permute-done | bytes 524320 | tf_op jit(solution)/shard_map/ppermute | solution.py:317
  34.4 0.8 norm_latitude.1
  35.2 5.2 %collective-permute-start.2 = (bf16[2,128,1024]{2,1,0:T(8,128)(2,1)S(1)}, bf16[2,128,1024]{2,1,0:T(8,128)(2,1)S(1)}, u32[]{:S(2)}, u32[]{:S(2)}) collective-permute-start(bf16[2,128,1024]{2,1,0:T(8,128)(2,1)S(1)} %collective-permute-done.refs_1_), channel_id=1, source_target_pairs={{0,256},{256,0},{1,257},{257,1},{2,258},{258,2},{3,259},{259,3},{4... | collective-permute-start | bytes 1572872 | tf_op jit(solution)/shard_map/ppermute | solution.py:309
  40.4 21.5 %all_to_all.25 = bf16[32,16,256]{2,1,0:T(8,128)(2,1)S(1)} all-to-all(bf16[32,16,256]{2,1,0:T(8,128)(2,1)S(1)} %get-tuple-element.34), channel_id=1, replica_groups=mesh['zl'=2,'y'=8,'core'=2,'xh'=2,'xl'=2,'zh'=4] {'zl','y','core'}, dimensions={0} | all-to-all | bytes 524288 | tf_op jit(solution)/shard_map/all_to_all | solution.py:348
  62.0 2.2 %collective-permute-start.4 = (bf16[2,2,128,1024]{3,2,1,0:T(8,128)(2,1)S(1)}, bf16[2,2,128,1024]{3,2,1,0:T(8,128)(2,1)S(1)}, u32[]{:S(2)}, u32[]{:S(2)}) collective-permute-start(bf16[2,2,128,1024]{3,2,1,0:T(8,128)(2,1)S(1)} %pad_maximum_fusion), channel_id=1, source_target_pairs={{0,4},{4,0},{1,5},{5,1},{2,6},{6,2},{3,7},{7,3},{8,12},{12,8},{9,1... | collective-permute-start | bytes 3145736 | tf_op jit(solution)/shard_map/ppermute | solution.py:309
  64.2 1.9 %spectral.1 = bf16[512,256]{1,0:T(8,128)(2,1)S(1)} custom-call(bf16[512,256]{1,0:T(8,128)(2,1)S(1)} %bitcast.17, bf16[512,512]{1,0:T(8,128)(2,1)S(1)} %copy-done.5, bf16[512,512]{1,0:T(8,128)(2,1)S(1)} %copy-done.4, bf16[432,256]{1,0:T(8,128)(2,1)S(1)} %constant_dynamic-update-slice_fusion.small_ref), custom_call_target="tpu_custom_call" | custom-call | tf_op jit(solution)/shard_map/spectral/pallas_call | solution.py:293
  66.1 4.6 %collective-permute-start.3 = (bf16[2,128,1024]{2,1,0:T(8,128)(2,1)S(1)}, bf16[2,128,1024]{2,1,0:T(8,128)(2,1)}, u32[]{:S(2)}, u32[]{:S(2)}) collective-permute-start(bf16[2,128,1024]{2,1,0:T(8,128)(2,1)S(1)} %collective-permute-done.2.refs_2_), channel_id=1, source_target_pairs={{256,1},{0,259},{257,2},{1,256},{258,3},{2,257},{259,0},{3,258},{2... | collective-permute-start | bytes 1572872 | tf_op jit(solution)/shard_map/ppermute | solution.py:317
  70.8 16.8 %all_to_all.26.rows_ref = bf16[32,16,256]{2,1,0:T(8,128)(2,1)S(1)} all-to-all(bf16[32,16,256]{2,1,0:T(8,128)(2,1)S(1)} %bitcast.18), channel_id=1, replica_groups=mesh['zl'=2,'y'=8,'core'=2,'xh'=2,'xl'=2,'zh'=4] {'zl','y','core'}, dimensions={0} | all-to-all | bytes 524288 | tf_op jit(solution)/shard_map/all_to_all | solution.py:365
  87.5 1.4 latitude_back.1
  88.9 5.3 %all-to-all-start.3 = ((bf16[16,2,64,128]{3,2,1,0:T(8,128)(2,1)}), bf16[16,2,64,128]{3,2,1,0:T(8,128)(2,1)S(1)}, u32[]{:S(2)}, u32[]{:S(2)}) async-start(bf16[16,2,64,128]{3,2,1,0:T(8,128)(2,1)} %bitcast.8), calls=%async_computation.3 | async-start | bytes 1048576 | tf_op jit(solution)/shard_map/all_to_all | solution.py:376
  94.2 3.4 %collective-permute-start.5 = (bf16[2,128,1024]{2,1,0:T(8,128)(2,1)}, bf16[2,128,1024]{2,1,0:T(8,128)(2,1)}, u32[]{:S(2)}, u32[]{:S(2)}) collective-permute-start(bf16[2,128,1024]{2,1,0:T(8,128)(2,1)} %collective-permute-done.3.refs_3_), channel_id=1, source_target_pairs={{0,4},{4,0},{1,5},{5,1},{2,6},{6,2},{3,7},{7,3},{8,12},{12,8},{9,1... | collective-permute-start | bytes 1572872 | tf_op jit(solution)/shard_map/ppermute | solution.py:309
  97.6 13.7 %all-to-all-done.3.mixed_ref.wide_ref = bf16[16,2,64,128]{3,2,1,0:T(8,128)(2,1)S(1)} async-done(((bf16[16,2,64,128]{3,2,1,0:T(8,128)(2,1)}), bf16[16,2,64,128]{3,2,1,0:T(8,128)(2,1)S(1)}, u32[]{:S(2)}, u32[]{:S(2)}) %all-to-all-start.3) | async-done | bytes 524320 | tf_op jit(solution)/shard_map/all_to_all | solution.py:376
  111.9 4.1 %collective-permute-start.6 = (bf16[1024,256]{1,0:T(8,128)(2,1)S(1)}, bf16[1024,256]{1,0:T(8,128)(2,1)S(1)}, u32[]{:S(2)}, u32[]{:S(2)}) collective-permute-start(bf16[1024,256]{1,0:T(8,128)(2,1)S(1)} %second_norm.1.refs_7_), channel_id=1, source_target_pairs={{0,16},{16,0},{1,17},{17,1},{2,18},{18,2},{3,19},{19,3},{4,20},{20... | collective-permute-start | bytes 1572872 | tf_op jit(solution)/shard_map/ppermute | solution.py:309
  116.0 1.5 collective-permute-done.6.refs_8_
  117.5 4.3 %channel_mlp.1 = (f32[1024,256]{1,0:T(8,128)S(1)}, bf16[1024,256]{1,0:T(8,128)(2,1)S(1)}) custom-call(bf16[2,128,1024]{2,1,0:T(8,128)(2,1)S(1)} %copy-done.1, bf16[2,128,1024]{2,1,0:T(8,128)(2,1)S(1)} %collective-permute-done.refs_1_, bf16[2,128,1024]{2,1,0:T(8,128)(2,1)S(1)} %collective-permute-done.2.refs_2_, ...), custom_call_target="tpu_custom_call" | custom-call | tf_op jit(solution)/shard_map/channel_mlp/pallas_call | solution.py:293
  121.8 2.3 %collective-permute-start.7 = (bf16[1024,256]{1,0:T(8,128)(2,1)S(1)}, bf16[1024,256]{1,0:T(8,128)(2,1)S(1)}, u32[]{:S(2)}, u32[]{:S(2)}) collective-permute-start(bf16[1024,256]{1,0:T(8,128)(2,1)S(1)} %get-tuple-element.48), channel_id=1, source_target_pairs={{0,16},{16,0},{1,17},{17,1},{2,18},{18,2},{3,19},{19,3},{4,20},{20... | collective-permute-start | bytes 1572872 | tf_op jit(solution)/shard_map/ppermute | solution.py:309
  124.1 1.5 %collective-permute-done.7.other_ref = bf16[1024,256]{1,0:T(8,128)(2,1)S(1)} collective-permute-done((bf16[1024,256]{1,0:T(8,128)(2,1)S(1)}, bf16[1024,256]{1,0:T(8,128)(2,1)S(1)}, u32[]{:S(2)}, u32[]{:S(2)}) %collective-permute-start.7) | collective-permute-done | bytes 524320 | tf_op jit(solution)/shard_map/ppermute | solution.py:309
  125.7 2.7 %collective-permute-start.8 = (bf16[512,256]{1,0:T(8,128)(2,1)S(1)}, bf16[512,256]{1,0:T(8,128)(2,1)S(1)}, u32[]{:S(2)}, u32[]{:S(2)}) collective-permute-start(bf16[512,256]{1,0:T(8,128)(2,1)S(1)} %get-tuple-element.50), channel_id=1, source_target_pairs={{0,8},{8,0},{1,9},{9,1},{2,10},{10,2},{3,11},{11,3},{4,12},{12,4},... | collective-permute-start | bytes 786440 | tf_op jit(solution)/shard_map/ppermute | solution.py:309
  128.4 8.2 %collective-permute-done.8.other_ref = bf16[512,256]{1,0:T(8,128)(2,1)S(1)} collective-permute-done((bf16[512,256]{1,0:T(8,128)(2,1)S(1)}, bf16[512,256]{1,0:T(8,128)(2,1)S(1)}, u32[]{:S(2)}, u32[]{:S(2)}) %collective-permute-start.8) | collective-permute-done | bytes 262176 | tf_op jit(solution)/shard_map/ppermute | solution.py:309
  136.7 13.3 %all_to_all.27 = bf16[8,2,64,128]{3,2,1,0:T(8,128)(2,1)S(1)} all-to-all(bf16[8,2,64,128]{3,2,1,0:T(8,128)(2,1)S(1)} %finish.1), channel_id=1, replica_groups=mesh['zl'=2,'y'=8,'core'=2,'xh'=2,'xl'=2,'zh'=4] {'xl','zh'}, dimensions={0} | all-to-all | bytes 524288 | tf_op jit(solution)/shard_map/all_to_all | solution.py:395
  (44 shorter events, 3.0 us)
Async XLA Ops:
  2.3 19.5 %collective-permute-start.1 = (bf16[2,128,1024]{2,1,0:T(8,128)(2,1)}, bf16[2,128,1024]{2,1,0:T(8,128)(2,1)S(1)}, u32[]{:S(2)}, u32[]{:S(2)}) collective-permute-start(bf16[2,128,1024]{2,1,0:T(8,128)(2,1)} %get-tuple-element.29.refs_0_), channel_id=1, source_target_pairs={{0,4},{4,0},{1,5},{5,1},{2,6},{6,2},{3,7},{7,3},{8,12},{12,8},{9,1... | collective-permute-start | bytes 1572872 | tf_op jit(solution)/shard_map/ppermute | solution.py:309
  6.2 27.5 %collective-permute-start = (bf16[2,128,1024]{2,1,0:T(8,128)(2,1)}, bf16[2,128,1024]{2,1,0:T(8,128)(2,1)S(1)}, u32[]{:S(2)}, u32[]{:S(2)}) collective-permute-start(bf16[2,128,1024]{2,1,0:T(8,128)(2,1)} %get-tuple-element.29.refs_0_), channel_id=1, source_target_pairs={{256,1},{0,259},{257,2},{1,256},{258,3},{2,257},{259,0},{3,258},{2... | collective-permute-start | bytes 1572872 | tf_op jit(solution)/shard_map/ppermute | solution.py:317
  16.9 4.1 %copy-start.8 = (bf16[64,256]{1,0:T(8,128)(2,1)S(1)}, bf16[64,256]{1,0:T(8,128)(2,1)}, u32[]{:S(2)}) copy-start(bf16[64,256]{1,0:T(8,128)(2,1)} %constant.15.clone) | copy-start | bytes 98308
  16.9 4.1 %copy-start.11 = (bf16[32,256]{1,0:T(8,128)(2,1)S(1)}, bf16[32,256]{1,0:T(8,128)(2,1)}, u32[]{:S(2)}) copy-start(bf16[32,256]{1,0:T(8,128)(2,1)} %constant.16.clone) | copy-start | bytes 49156
  16.9 4.1 %copy-start.10 = (bf16[32,256]{1,0:T(8,128)(2,1)S(1)}, bf16[32,256]{1,0:T(8,128)(2,1)}, u32[]{:S(2)}) copy-start(bf16[32,256]{1,0:T(8,128)(2,1)} %constant.17.clone) | copy-start | bytes 49156
  16.9 4.1 %copy-start.9 = (bf16[32,256]{1,0:T(8,128)(2,1)S(1)}, bf16[32,256]{1,0:T(8,128)(2,1)}, u32[]{:S(2)}) copy-start(bf16[32,256]{1,0:T(8,128)(2,1)} %constant.18.clone) | copy-start | bytes 49156
  17.0 4.1 %copy-start.6 = (bf16[2,64,64]{2,1,0:T(8,128)(2,1)S(1)}, bf16[2,64,64]{2,1,0:T(8,128)(2,1)}, u32[]{:S(2)}) copy-start(bf16[2,64,64]{2,1,0:T(8,128)(2,1)} %param.15) | copy-start | bytes 49156
  17.0 4.1 %copy-start.7 = (bf16[2,64,64]{2,1,0:T(8,128)(2,1)S(1)}, bf16[2,64,64]{2,1,0:T(8,128)(2,1)}, u32[]{:S(2)}) copy-start(bf16[2,64,64]{2,1,0:T(8,128)(2,1)} %param.16) | copy-start | bytes 49156
  17.0 17.4 %all-to-all-start = ((f32[16,40,128]{2,1,0:T(8,128)}), f32[16,40,128]{2,1,0:T(8,128)S(1)}, u32[]{:S(2)}, u32[]{:S(2)}) async-start(f32[16,40,128]{2,1,0:T(8,128)} %get-tuple-element.28), calls=%async_computation | async-start | bytes 655360 | tf_op jit(solution)/shard_map/all_to_all | solution.py:325
  21.0 13.4 %copy-start = (bf16[128,16,64]{0,2,1:T(8,128)(2,1)S(1)}, bf16[128,16,64]{0,2,1:T(8,128)(2,1)}, u32[]{:S(2)}) copy-start(bf16[128,16,64]{0,2,1:T(8,128)(2,1)} %param.13) | copy-start | bytes 786436
  21.1 0.7 copy-start.12
  21.8 13.4 %copy-start.2 = (bf16[2,128,1024]{2,1,0:T(8,128)(2,1)}, bf16[2,128,1024]{2,1,0:T(8,128)(2,1)S(1)}, u32[]{:S(2)}) copy-start(bf16[2,128,1024]{2,1,0:T(8,128)(2,1)S(1)} %collective-permute-done.1.refs_4_) | copy-start | bytes 1572868
  35.2 26.7 %collective-permute-start.2 = (bf16[2,128,1024]{2,1,0:T(8,128)(2,1)S(1)}, bf16[2,128,1024]{2,1,0:T(8,128)(2,1)S(1)}, u32[]{:S(2)}, u32[]{:S(2)}) collective-permute-start(bf16[2,128,1024]{2,1,0:T(8,128)(2,1)S(1)} %collective-permute-done.refs_1_), channel_id=1, source_target_pairs={{0,256},{256,0},{1,257},{257,1},{2,258},{258,2},{3,259},{259,3},{4... | collective-permute-start | bytes 1572872 | tf_op jit(solution)/shard_map/ppermute | solution.py:309
  61.9 2.3 %copy-start.4 = (bf16[512,512]{1,0:T(8,128)(2,1)S(1)}, bf16[512,512]{1,0:T(8,128)(2,1)}, u32[]{:S(2)}) copy-start(bf16[512,512]{1,0:T(8,128)(2,1)} %constant.20.clone.inverse_ref) | copy-start | bytes 1572868
  61.9 2.3 %copy-start.5 = (bf16[512,512]{1,0:T(8,128)(2,1)S(1)}, bf16[512,512]{1,0:T(8,128)(2,1)}, u32[]{:S(2)}) copy-start(bf16[512,512]{1,0:T(8,128)(2,1)} %constant.19.clone.lon_ref) | copy-start | bytes 1572868
  62.0 25.5 %collective-permute-start.4 = (bf16[2,2,128,1024]{3,2,1,0:T(8,128)(2,1)S(1)}, bf16[2,2,128,1024]{3,2,1,0:T(8,128)(2,1)S(1)}, u32[]{:S(2)}, u32[]{:S(2)}) collective-permute-start(bf16[2,2,128,1024]{3,2,1,0:T(8,128)(2,1)S(1)} %pad_maximum_fusion), channel_id=1, source_target_pairs={{0,4},{4,0},{1,5},{5,1},{2,6},{6,2},{3,7},{7,3},{8,12},{12,8},{9,1... | collective-permute-start | bytes 3145736 | tf_op jit(solution)/shard_map/ppermute | solution.py:309
  66.1 21.4 %collective-permute-start.3 = (bf16[2,128,1024]{2,1,0:T(8,128)(2,1)S(1)}, bf16[2,128,1024]{2,1,0:T(8,128)(2,1)}, u32[]{:S(2)}, u32[]{:S(2)}) collective-permute-start(bf16[2,128,1024]{2,1,0:T(8,128)(2,1)S(1)} %collective-permute-done.2.refs_2_), channel_id=1, source_target_pairs={{256,1},{0,259},{257,2},{1,256},{258,3},{2,257},{259,0},{3,258},{2... | collective-permute-start | bytes 1572872 | tf_op jit(solution)/shard_map/ppermute | solution.py:317
  88.9 22.4 %all-to-all-start.3 = ((bf16[16,2,64,128]{3,2,1,0:T(8,128)(2,1)}), bf16[16,2,64,128]{3,2,1,0:T(8,128)(2,1)S(1)}, u32[]{:S(2)}, u32[]{:S(2)}) async-start(bf16[16,2,64,128]{3,2,1,0:T(8,128)(2,1)} %bitcast.8), calls=%async_computation.3 | async-start | bytes 1048576 | tf_op jit(solution)/shard_map/all_to_all | solution.py:376
  94.2 23.3 %copy-start.1 = (bf16[2,128,1024]{2,1,0:T(8,128)(2,1)S(1)}, bf16[2,128,1024]{2,1,0:T(8,128)(2,1)}, u32[]{:S(2)}) copy-start(bf16[2,128,1024]{2,1,0:T(8,128)(2,1)} %get-tuple-element.29.refs_0_) | copy-start | bytes 1572868
  94.2 21.8 %collective-permute-start.5 = (bf16[2,128,1024]{2,1,0:T(8,128)(2,1)}, bf16[2,128,1024]{2,1,0:T(8,128)(2,1)}, u32[]{:S(2)}, u32[]{:S(2)}) collective-permute-start(bf16[2,128,1024]{2,1,0:T(8,128)(2,1)} %collective-permute-done.3.refs_3_), channel_id=1, source_target_pairs={{0,4},{4,0},{1,5},{5,1},{2,6},{6,2},{3,7},{7,3},{8,12},{12,8},{9,1... | collective-permute-start | bytes 1572872 | tf_op jit(solution)/shard_map/ppermute | solution.py:309
  111.3 6.2 %copy-start.3 = (bf16[2,128,1024]{2,1,0:T(8,128)(2,1)S(1)}, bf16[2,128,1024]{2,1,0:T(8,128)(2,1)}, u32[]{:S(2)}) copy-start(bf16[2,128,1024]{2,1,0:T(8,128)(2,1)} %copy-done.2) | copy-start | bytes 1572868
  111.9 5.7 %collective-permute-start.6 = (bf16[1024,256]{1,0:T(8,128)(2,1)S(1)}, bf16[1024,256]{1,0:T(8,128)(2,1)S(1)}, u32[]{:S(2)}, u32[]{:S(2)}) collective-permute-start(bf16[1024,256]{1,0:T(8,128)(2,1)S(1)} %second_norm.1.refs_7_), channel_id=1, source_target_pairs={{0,16},{16,0},{1,17},{17,1},{2,18},{18,2},{3,19},{19,3},{4,20},{20... | collective-permute-start | bytes 1572872 | tf_op jit(solution)/shard_map/ppermute | solution.py:309
  121.8 3.8 %collective-permute-start.7 = (bf16[1024,256]{1,0:T(8,128)(2,1)S(1)}, bf16[1024,256]{1,0:T(8,128)(2,1)S(1)}, u32[]{:S(2)}, u32[]{:S(2)}) collective-permute-start(bf16[1024,256]{1,0:T(8,128)(2,1)S(1)} %get-tuple-element.48), channel_id=1, source_target_pairs={{0,16},{16,0},{1,17},{17,1},{2,18},{18,2},{3,19},{19,3},{4,20},{20... | collective-permute-start | bytes 1572872 | tf_op jit(solution)/shard_map/ppermute | solution.py:309
  125.7 10.9 %collective-permute-start.8 = (bf16[512,256]{1,0:T(8,128)(2,1)S(1)}, bf16[512,256]{1,0:T(8,128)(2,1)S(1)}, u32[]{:S(2)}, u32[]{:S(2)}) collective-permute-start(bf16[512,256]{1,0:T(8,128)(2,1)S(1)} %get-tuple-element.50), channel_id=1, source_target_pairs={{0,8},{8,0},{1,9},{9,1},{2,10},{10,2},{3,11},{11,3},{4,12},{12,4},... | collective-permute-start | bytes 786440 | tf_op jit(solution)/shard_map/ppermute | solution.py:309

commit v4 on v3

--- a/solution.py
+++ b/solution.py
@@ -281,7 +281,7 @@
     xh = lax.axis_index("xh")
     for d in range(8):
         rows = slice(d * 64, d * 64 + 64)
-        branch = keep_ref[rows] + other_ref[rows].astype(F32)
+        branch = keep_ref[rows] + other_ref[1 - xh, rows].astype(F32)
         for w in range(2):
             sums = wide_ref[xh * 8 + d, w].astype(F32) + branch[:, w * 128 : w * 128 + 128]
             out_ref[d, w] = sums.astype(BF16)
@@ -391,7 +391,7 @@
         "core_sum",
         (own_out, swap(other_out, "core")),
     )
-    result = call(finish_kernel, shape((8, 2, 64, 128)), [], "finish", (wide, keep, swap(send, "xh")))
+    result = call(finish_kernel, shape((8, 2, 64, 128)), [], "finish", (wide, keep, lax.all_gather(send, "xh", axis=0)))
     result = lax.all_to_all(lax.optimization_barrier(result), ("xl", "zh"), 0, 0)
     return result.reshape(16, 64, 128).transpose(2, 0, 1)
 

time: 153 us -> 151 us (0.987)
  blocking collectives: 51.6 us -> 61.3 us
  waiting for transfers between devices: 37.5 us -> 29.3 us
  starting transfers between devices: 48.4 us -> 45.7 us
    all_gather x0 -> x1, blocking collectives: none -> 9.7 us  [per_device(): lax.all_gather(send, 'xh', axis=0)]
    ppermute x7 -> x6, waiting for transfers between devices: 11.3 us -> 3.03 us  [swap(): return lax.ppermute(values, axis, [(0, 1), (1, 0)])]
    ppermute x7 -> x6, starting transfers between devices: 23.8 us -> 21.1 us  [swap(): return lax.ppermute(values, axis, [(0, 1), (1, 0)])]
  transfers between devices with their start and end apart: 11 -> 10, of which waited for: 6 -> 5; matrix products, arithmetic and copies ran while one was open for 0% -> 0% of each run, Pallas kernels for 2% -> 2%
where the time goes in v4:
time: 151 us; the launch traced here: 149 us
  blocking collectives  61.3 us (41%)
  starting transfers between devices  45.7 us (30%)
  waiting for transfers between devices  29.3 us (19%)
  Pallas kernels  11.3 us (7%)
    all_to_all x1, blocking collectives, per_device(): rows = lax.all_to_all(rows, LON_AXES, 0, 0)  21.5 us
    ppermute x6, starting transfers between devices, swap(): return lax.ppermute(values, axis, [(0, 1), (1, 0)])  21.1 us
    all_to_all x1, blocking collectives, per_device(): back = lax.all_to_all(back, LON_AXES, 0, 0)  16.8 us
    ppermute x2, starting transfers between devices, next_pair(): return lax.ppermute(values, ('zl', 'zh'), pairs)  15.3 us
    all_to_all x1, waiting for transfers between devices, per_device(): wide = lax.all_to_all(mixed.reshape(16, 2, 64, 128), CH_AXES, 0, 0)  13.7 us
    all_to_all x1, blocking collectives, per_device(): lax.all_to_all(lax.optimization_barrier(result), ('xl', 'zh'), 0, 0)  13.3 us
    ppermute x2, waiting for transfers between devices, next_pair(): return lax.ppermute(values, ('zl', 'zh'), pairs)  11.9 us
    all_gather x1, blocking collectives, per_device(): lax.all_gather(send, 'xh', axis=0)  9.7 us
  transfers between devices with their start and end apart: 10, of which 5 were waited for; matrix products, arithmetic and copies ran while one was open for 0% of the time, Pallas kernels for 2%

profile of v4, /device:TPU:1, one launch (start us, length us, event | category | flops | bytes accessed | tf_op | source)
XLA Modules:
  0.0 149.5 jit_solution(14714780151576415088)
XLA Ops:
  0.0 2.3 %setup.1 = (bf16[2,128,1024]{2,1,0:T(8,128)(2,1)}, f32[16,40,128]{2,1,0:T(8,128)}) custom-call(bf16[1024,256]{1,0:T(8,128)(2,1)} %up_ref.1, bf16[256,1024]{1,0:T(8,128)(2,1)} %down_ref.1, bf16[16,64,128]{2,1,0:T(8,128)(2,1)} %bitcast.13, bf16[64]{0:T(256)(128)(2,1)} %gain_ref.1), custom_call_target="tpu_custom_call" | custom-call | tf_op jit(solution)/shard_map/setup/pallas_call | solution.py:143
  2.3 4.0 %collective-permute-start.1 = (bf16[2,128,1024]{2,1,0:T(8,128)(2,1)}, bf16[2,128,1024]{2,1,0:T(8,128)(2,1)S(1)}, u32[]{:S(2)}, u32[]{:S(2)}) collective-permute-start(bf16[2,128,1024]{2,1,0:T(8,128)(2,1)} %get-tuple-element.29.refs_0_), channel_id=1, source_target_pairs={{0,4},{4,0},{1,5},{5,1},{2,6},{6,2},{3,7},{7,3},{8,12},{12,8},{9,1... | collective-permute-start | bytes 1572872 | tf_op jit(solution)/shard_map/ppermute | solution.py:309
  6.2 10.7 %collective-permute-start = (bf16[2,128,1024]{2,1,0:T(8,128)(2,1)}, bf16[2,128,1024]{2,1,0:T(8,128)(2,1)S(1)}, u32[]{:S(2)}, u32[]{:S(2)}) collective-permute-start(bf16[2,128,1024]{2,1,0:T(8,128)(2,1)} %get-tuple-element.29.refs_0_), channel_id=1, source_target_pairs={{256,1},{0,259},{257,2},{1,256},{258,3},{2,257},{259,0},{3,258},{2... | collective-permute-start | bytes 1572872 | tf_op jit(solution)/shard_map/ppermute | solution.py:317
  17.0 4.0 %all-to-all-start = ((f32[16,40,128]{2,1,0:T(8,128)}), f32[16,40,128]{2,1,0:T(8,128)S(1)}, u32[]{:S(2)}, u32[]{:S(2)}) async-start(f32[16,40,128]{2,1,0:T(8,128)} %get-tuple-element.28), calls=%async_computation | async-start | bytes 655360 | tf_op jit(solution)/shard_map/all_to_all | solution.py:325
  21.8 11.9 %collective-permute-done.refs_1_ = bf16[2,128,1024]{2,1,0:T(8,128)(2,1)S(1)} collective-permute-done((bf16[2,128,1024]{2,1,0:T(8,128)(2,1)}, bf16[2,128,1024]{2,1,0:T(8,128)(2,1)S(1)}, u32[]{:S(2)}, u32[]{:S(2)}) %collective-permute-start) | collective-permute-done | bytes 524320 | tf_op jit(solution)/shard_map/ppermute | solution.py:317
  34.4 0.8 norm_latitude.1
  35.2 5.2 %collective-permute-start.2 = (bf16[2,128,1024]{2,1,0:T(8,128)(2,1)S(1)}, bf16[2,128,1024]{2,1,0:T(8,128)(2,1)S(1)}, u32[]{:S(2)}, u32[]{:S(2)}) collective-permute-start(bf16[2,128,1024]{2,1,0:T(8,128)(2,1)S(1)} %collective-permute-done.refs_1_), channel_id=1, source_target_pairs={{0,256},{256,0},{1,257},{257,1},{2,258},{258,2},{3,259},{259,3},{4... | collective-permute-start | bytes 1572872 | tf_op jit(solution)/shard_map/ppermute | solution.py:309
  40.4 21.5 %all_to_all.25 = bf16[32,16,256]{2,1,0:T(8,128)(2,1)S(1)} all-to-all(bf16[32,16,256]{2,1,0:T(8,128)(2,1)S(1)} %get-tuple-element.34), channel_id=1, replica_groups=mesh['zl'=2,'y'=8,'core'=2,'xh'=2,'xl'=2,'zh'=4] {'zl','y','core'}, dimensions={0} | all-to-all | bytes 524288 | tf_op jit(solution)/shard_map/all_to_all | solution.py:348
  62.0 2.2 %collective-permute-start.4 = (bf16[2,2,128,1024]{3,2,1,0:T(8,128)(2,1)S(1)}, bf16[2,2,128,1024]{3,2,1,0:T(8,128)(2,1)S(1)}, u32[]{:S(2)}, u32[]{:S(2)}) collective-permute-start(bf16[2,2,128,1024]{3,2,1,0:T(8,128)(2,1)S(1)} %pad_maximum_fusion), channel_id=1, source_target_pairs={{0,4},{4,0},{1,5},{5,1},{2,6},{6,2},{3,7},{7,3},{8,12},{12,8},{9,1... | collective-permute-start | bytes 3145736 | tf_op jit(solution)/shard_map/ppermute | solution.py:309
  64.2 1.9 %spectral.1 = bf16[512,256]{1,0:T(8,128)(2,1)S(1)} custom-call(bf16[512,256]{1,0:T(8,128)(2,1)S(1)} %bitcast.19, bf16[512,512]{1,0:T(8,128)(2,1)S(1)} %copy-done.5, bf16[512,512]{1,0:T(8,128)(2,1)S(1)} %copy-done.4, bf16[432,256]{1,0:T(8,128)(2,1)S(1)} %constant_dynamic-update-slice_fusion.small_ref), custom_call_target="tpu_custom_call" | custom-call | tf_op jit(solution)/shard_map/spectral/pallas_call | solution.py:293
  66.1 4.6 %collective-permute-start.3 = (bf16[2,128,1024]{2,1,0:T(8,128)(2,1)S(1)}, bf16[2,128,1024]{2,1,0:T(8,128)(2,1)}, u32[]{:S(2)}, u32[]{:S(2)}) collective-permute-start(bf16[2,128,1024]{2,1,0:T(8,128)(2,1)S(1)} %collective-permute-done.2.refs_2_), channel_id=1, source_target_pairs={{256,1},{0,259},{257,2},{1,256},{258,3},{2,257},{259,0},{3,258},{2... | collective-permute-start | bytes 1572872 | tf_op jit(solution)/shard_map/ppermute | solution.py:317
  70.8 16.8 %all_to_all.26.rows_ref = bf16[32,16,256]{2,1,0:T(8,128)(2,1)S(1)} all-to-all(bf16[32,16,256]{2,1,0:T(8,128)(2,1)S(1)} %bitcast.20), channel_id=1, replica_groups=mesh['zl'=2,'y'=8,'core'=2,'xh'=2,'xl'=2,'zh'=4] {'zl','y','core'}, dimensions={0} | all-to-all | bytes 524288 | tf_op jit(solution)/shard_map/all_to_all | solution.py:365
  87.5 1.4 latitude_back.1
  88.9 5.3 %all-to-all-start.3 = ((bf16[16,2,64,128]{3,2,1,0:T(8,128)(2,1)}), bf16[16,2,64,128]{3,2,1,0:T(8,128)(2,1)S(1)}, u32[]{:S(2)}, u32[]{:S(2)}) async-start(bf16[16,2,64,128]{3,2,1,0:T(8,128)(2,1)} %bitcast.8), calls=%async_computation.3 | async-start | bytes 1048576 | tf_op jit(solution)/shard_map/all_to_all | solution.py:376
  94.2 3.4 %collective-permute-start.5 = (bf16[2,128,1024]{2,1,0:T(8,128)(2,1)}, bf16[2,128,1024]{2,1,0:T(8,128)(2,1)}, u32[]{:S(2)}, u32[]{:S(2)}) collective-permute-start(bf16[2,128,1024]{2,1,0:T(8,128)(2,1)} %collective-permute-done.3.refs_3_), channel_id=1, source_target_pairs={{0,4},{4,0},{1,5},{5,1},{2,6},{6,2},{3,7},{7,3},{8,12},{12,8},{9,1... | collective-permute-start | bytes 1572872 | tf_op jit(solution)/shard_map/ppermute | solution.py:309
  97.6 13.7 %all-to-all-done.3.mixed_ref.wide_ref = bf16[16,2,64,128]{3,2,1,0:T(8,128)(2,1)S(1)} async-done(((bf16[16,2,64,128]{3,2,1,0:T(8,128)(2,1)}), bf16[16,2,64,128]{3,2,1,0:T(8,128)(2,1)S(1)}, u32[]{:S(2)}, u32[]{:S(2)}) %all-to-all-start.3) | async-done | bytes 524320 | tf_op jit(solution)/shard_map/all_to_all | solution.py:376
  111.9 4.1 %collective-permute-start.6 = (bf16[1024,256]{1,0:T(8,128)(2,1)S(1)}, bf16[1024,256]{1,0:T(8,128)(2,1)S(1)}, u32[]{:S(2)}, u32[]{:S(2)}) collective-permute-start(bf16[1024,256]{1,0:T(8,128)(2,1)S(1)} %second_norm.1.refs_7_), channel_id=1, source_target_pairs={{0,16},{16,0},{1,17},{17,1},{2,18},{18,2},{3,19},{19,3},{4,20},{20... | collective-permute-start | bytes 1572872 | tf_op jit(solution)/shard_map/ppermute | solution.py:309
  116.0 1.5 %collective-permute-done.6.refs_8_ = bf16[1024,256]{1,0:T(8,128)(2,1)S(1)} collective-permute-done((bf16[1024,256]{1,0:T(8,128)(2,1)S(1)}, bf16[1024,256]{1,0:T(8,128)(2,1)S(1)}, u32[]{:S(2)}, u32[]{:S(2)}) %collective-permute-start.6) | collective-permute-done | bytes 524320 | tf_op jit(solution)/shard_map/ppermute | solution.py:309
  117.5 4.3 %channel_mlp.1 = (f32[1024,256]{1,0:T(8,128)S(1)}, bf16[1024,256]{1,0:T(8,128)(2,1)S(1)}) custom-call(bf16[2,128,1024]{2,1,0:T(8,128)(2,1)S(1)} %copy-done.1, bf16[2,128,1024]{2,1,0:T(8,128)(2,1)S(1)} %collective-permute-done.refs_1_, bf16[2,128,1024]{2,1,0:T(8,128)(2,1)S(1)} %collective-permute-done.2.refs_2_, ...), custom_call_target="tpu_custom_call" | custom-call | tf_op jit(solution)/shard_map/channel_mlp/pallas_call | solution.py:293
  121.8 2.3 %collective-permute-start.7 = (bf16[1024,256]{1,0:T(8,128)(2,1)S(1)}, bf16[1024,256]{1,0:T(8,128)(2,1)S(1)}, u32[]{:S(2)}, u32[]{:S(2)}) collective-permute-start(bf16[1024,256]{1,0:T(8,128)(2,1)S(1)} %get-tuple-element.48), channel_id=1, source_target_pairs={{0,16},{16,0},{1,17},{17,1},{2,18},{18,2},{3,19},{19,3},{4,20},{20... | collective-permute-start | bytes 1572872 | tf_op jit(solution)/shard_map/ppermute | solution.py:309
  124.1 1.5 %collective-permute-done.7.other_ref = bf16[1024,256]{1,0:T(8,128)(2,1)S(1)} collective-permute-done((bf16[1024,256]{1,0:T(8,128)(2,1)S(1)}, bf16[1024,256]{1,0:T(8,128)(2,1)S(1)}, u32[]{:S(2)}, u32[]{:S(2)}) %collective-permute-start.7) | collective-permute-done | bytes 524320 | tf_op jit(solution)/shard_map/ppermute | solution.py:309
  125.7 9.7 %all-gather = bf16[1024,256]{1,0:T(8,128)(2,1)S(1)} all-gather(bf16[512,256]{1,0:T(8,128)(2,1)S(1)} %get-tuple-element.50), channel_id=2, replica_groups=mesh['zl'=2,'y'=8,'core'=2,'xh'=2,'xl'=2,'zh'=4] {'xh'}, dimensions={0}, use_global_device_ids=true | all-gather | bytes 786432 | tf_op jit(solution)/shard_map/all_gather | solution.py:394
  135.5 13.3 %all_to_all.27 = bf16[8,2,64,128]{3,2,1,0:T(8,128)(2,1)S(1)} all-to-all(bf16[8,2,64,128]{3,2,1,0:T(8,128)(2,1)S(1)} %finish.1), channel_id=1, replica_groups=mesh['zl'=2,'y'=8,'core'=2,'xh'=2,'xl'=2,'zh'=4] {'xl','zh'}, dimensions={0} | all-to-all | bytes 524288 | tf_op jit(solution)/shard_map/all_to_all | solution.py:395
  148.8 0.7 copy.21
  (43 shorter events, 2.3 us)
Async XLA Ops:
  2.3 19.5 %collective-permute-start.1 = (bf16[2,128,1024]{2,1,0:T(8,128)(2,1)}, bf16[2,128,1024]{2,1,0:T(8,128)(2,1)S(1)}, u32[]{:S(2)}, u32[]{:S(2)}) collective-permute-start(bf16[2,128,1024]{2,1,0:T(8,128)(2,1)} %get-tuple-element.29.refs_0_), channel_id=1, source_target_pairs={{0,4},{4,0},{1,5},{5,1},{2,6},{6,2},{3,7},{7,3},{8,12},{12,8},{9,1... | collective-permute-start | bytes 1572872 | tf_op jit(solution)/shard_map/ppermute | solution.py:309
  6.2 27.5 %collective-permute-start = (bf16[2,128,1024]{2,1,0:T(8,128)(2,1)}, bf16[2,128,1024]{2,1,0:T(8,128)(2,1)S(1)}, u32[]{:S(2)}, u32[]{:S(2)}) collective-permute-start(bf16[2,128,1024]{2,1,0:T(8,128)(2,1)} %get-tuple-element.29.refs_0_), channel_id=1, source_target_pairs={{256,1},{0,259},{257,2},{1,256},{258,3},{2,257},{259,0},{3,258},{2... | collective-permute-start | bytes 1572872 | tf_op jit(solution)/shard_map/ppermute | solution.py:317
  16.9 4.1 %copy-start.8 = (bf16[64,256]{1,0:T(8,128)(2,1)S(1)}, bf16[64,256]{1,0:T(8,128)(2,1)}, u32[]{:S(2)}) copy-start(bf16[64,256]{1,0:T(8,128)(2,1)} %constant.15.clone) | copy-start | bytes 98308
  16.9 4.1 %copy-start.11 = (bf16[32,256]{1,0:T(8,128)(2,1)S(1)}, bf16[32,256]{1,0:T(8,128)(2,1)}, u32[]{:S(2)}) copy-start(bf16[32,256]{1,0:T(8,128)(2,1)} %constant.16.clone) | copy-start | bytes 49156
  16.9 4.1 %copy-start.10 = (bf16[32,256]{1,0:T(8,128)(2,1)S(1)}, bf16[32,256]{1,0:T(8,128)(2,1)}, u32[]{:S(2)}) copy-start(bf16[32,256]{1,0:T(8,128)(2,1)} %constant.17.clone) | copy-start | bytes 49156
  17.0 4.1 %copy-start.9 = (bf16[32,256]{1,0:T(8,128)(2,1)S(1)}, bf16[32,256]{1,0:T(8,128)(2,1)}, u32[]{:S(2)}) copy-start(bf16[32,256]{1,0:T(8,128)(2,1)} %constant.18.clone) | copy-start | bytes 49156
  17.0 4.1 %copy-start.6 = (bf16[2,64,64]{2,1,0:T(8,128)(2,1)S(1)}, bf16[2,64,64]{2,1,0:T(8,128)(2,1)}, u32[]{:S(2)}) copy-start(bf16[2,64,64]{2,1,0:T(8,128)(2,1)} %param.15) | copy-start | bytes 49156
  17.0 4.1 %copy-start.7 = (bf16[2,64,64]{2,1,0:T(8,128)(2,1)S(1)}, bf16[2,64,64]{2,1,0:T(8,128)(2,1)}, u32[]{:S(2)}) copy-start(bf16[2,64,64]{2,1,0:T(8,128)(2,1)} %param.16) | copy-start | bytes 49156
  17.0 17.4 %all-to-all-start = ((f32[16,40,128]{2,1,0:T(8,128)}), f32[16,40,128]{2,1,0:T(8,128)S(1)}, u32[]{:S(2)}, u32[]{:S(2)}) async-start(f32[16,40,128]{2,1,0:T(8,128)} %get-tuple-element.28), calls=%async_computation | async-start | bytes 655360 | tf_op jit(solution)/shard_map/all_to_all | solution.py:325
  21.0 13.4 %copy-start = (bf16[128,16,64]{0,2,1:T(8,128)(2,1)S(1)}, bf16[128,16,64]{0,2,1:T(8,128)(2,1)}, u32[]{:S(2)}) copy-start(bf16[128,16,64]{0,2,1:T(8,128)(2,1)} %param.13) | copy-start | bytes 786436
  21.1 0.7 copy-start.12
  21.8 13.4 %copy-start.2 = (bf16[2,128,1024]{2,1,0:T(8,128)(2,1)}, bf16[2,128,1024]{2,1,0:T(8,128)(2,1)S(1)}, u32[]{:S(2)}) copy-start(bf16[2,128,1024]{2,1,0:T(8,128)(2,1)S(1)} %collective-permute-done.1.refs_4_) | copy-start | bytes 1572868
  35.2 26.7 %collective-permute-start.2 = (bf16[2,128,1024]{2,1,0:T(8,128)(2,1)S(1)}, bf16[2,128,1024]{2,1,0:T(8,128)(2,1)S(1)}, u32[]{:S(2)}, u32[]{:S(2)}) collective-permute-start(bf16[2,128,1024]{2,1,0:T(8,128)(2,1)S(1)} %collective-permute-done.refs_1_), channel_id=1, source_target_pairs={{0,256},{256,0},{1,257},{257,1},{2,258},{258,2},{3,259},{259,3},{4... | collective-permute-start | bytes 1572872 | tf_op jit(solution)/shard_map/ppermute | solution.py:309
  61.9 2.3 %copy-start.4 = (bf16[512,512]{1,0:T(8,128)(2,1)S(1)}, bf16[512,512]{1,0:T(8,128)(2,1)}, u32[]{:S(2)}) copy-start(bf16[512,512]{1,0:T(8,128)(2,1)} %constant.20.clone.inverse_ref) | copy-start | bytes 1572868
  61.9 2.3 %copy-start.5 = (bf16[512,512]{1,0:T(8,128)(2,1)S(1)}, bf16[512,512]{1,0:T(8,128)(2,1)}, u32[]{:S(2)}) copy-start(bf16[512,512]{1,0:T(8,128)(2,1)} %constant.19.clone.lon_ref) | copy-start | bytes 1572868
  62.0 25.5 %collective-permute-start.4 = (bf16[2,2,128,1024]{3,2,1,0:T(8,128)(2,1)S(1)}, bf16[2,2,128,1024]{3,2,1,0:T(8,128)(2,1)S(1)}, u32[]{:S(2)}, u32[]{:S(2)}) collective-permute-start(bf16[2,2,128,1024]{3,2,1,0:T(8,128)(2,1)S(1)} %pad_maximum_fusion), channel_id=1, source_target_pairs={{0,4},{4,0},{1,5},{5,1},{2,6},{6,2},{3,7},{7,3},{8,12},{12,8},{9,1... | collective-permute-start | bytes 3145736 | tf_op jit(solution)/shard_map/ppermute | solution.py:309
  66.1 21.4 %collective-permute-start.3 = (bf16[2,128,1024]{2,1,0:T(8,128)(2,1)S(1)}, bf16[2,128,1024]{2,1,0:T(8,128)(2,1)}, u32[]{:S(2)}, u32[]{:S(2)}) collective-permute-start(bf16[2,128,1024]{2,1,0:T(8,128)(2,1)S(1)} %collective-permute-done.2.refs_2_), channel_id=1, source_target_pairs={{256,1},{0,259},{257,2},{1,256},{258,3},{2,257},{259,0},{3,258},{2... | collective-permute-start | bytes 1572872 | tf_op jit(solution)/shard_map/ppermute | solution.py:317
  88.9 22.4 %all-to-all-start.3 = ((bf16[16,2,64,128]{3,2,1,0:T(8,128)(2,1)}), bf16[16,2,64,128]{3,2,1,0:T(8,128)(2,1)S(1)}, u32[]{:S(2)}, u32[]{:S(2)}) async-start(bf16[16,2,64,128]{3,2,1,0:T(8,128)(2,1)} %bitcast.8), calls=%async_computation.3 | async-start | bytes 1048576 | tf_op jit(solution)/shard_map/all_to_all | solution.py:376
  94.2 23.3 %copy-start.1 = (bf16[2,128,1024]{2,1,0:T(8,128)(2,1)S(1)}, bf16[2,128,1024]{2,1,0:T(8,128)(2,1)}, u32[]{:S(2)}) copy-start(bf16[2,128,1024]{2,1,0:T(8,128)(2,1)} %get-tuple-element.29.refs_0_) | copy-start | bytes 1572868
  94.2 21.8 %collective-permute-start.5 = (bf16[2,128,1024]{2,1,0:T(8,128)(2,1)}, bf16[2,128,1024]{2,1,0:T(8,128)(2,1)}, u32[]{:S(2)}, u32[]{:S(2)}) collective-permute-start(bf16[2,128,1024]{2,1,0:T(8,128)(2,1)} %collective-permute-done.3.refs_3_), channel_id=1, source_target_pairs={{0,4},{4,0},{1,5},{5,1},{2,6},{6,2},{3,7},{7,3},{8,12},{12,8},{9,1... | collective-permute-start | bytes 1572872 | tf_op jit(solution)/shard_map/ppermute | solution.py:309
  111.3 6.2 %copy-start.3 = (bf16[2,128,1024]{2,1,0:T(8,128)(2,1)S(1)}, bf16[2,128,1024]{2,1,0:T(8,128)(2,1)}, u32[]{:S(2)}) copy-start(bf16[2,128,1024]{2,1,0:T(8,128)(2,1)} %copy-done.2) | copy-start | bytes 1572868
  111.9 5.7 %collective-permute-start.6 = (bf16[1024,256]{1,0:T(8,128)(2,1)S(1)}, bf16[1024,256]{1,0:T(8,128)(2,1)S(1)}, u32[]{:S(2)}, u32[]{:S(2)}) collective-permute-start(bf16[1024,256]{1,0:T(8,128)(2,1)S(1)} %second_norm.1.refs_7_), channel_id=1, source_target_pairs={{0,16},{16,0},{1,17},{17,1},{2,18},{18,2},{3,19},{19,3},{4,20},{20... | collective-permute-start | bytes 1572872 | tf_op jit(solution)/shard_map/ppermute | solution.py:309
  121.8 3.8 %collective-permute-start.7 = (bf16[1024,256]{1,0:T(8,128)(2,1)S(1)}, bf16[1024,256]{1,0:T(8,128)(2,1)S(1)}, u32[]{:S(2)}, u32[]{:S(2)}) collective-permute-start(bf16[1024,256]{1,0:T(8,128)(2,1)S(1)} %get-tuple-element.48), channel_id=1, source_target_pairs={{0,16},{16,0},{1,17},{17,1},{2,18},{18,2},{3,19},{19,3},{4,20},{20... | collective-permute-start | bytes 1572872 | tf_op jit(solution)/shard_map/ppermute | solution.py:309

commit v5 on v4

--- a/solution.py
+++ b/solution.py
@@ -269,6 +269,24 @@
     other_out[...] = total[:, 256:].astype(BF16)
 
 
+def bring_kernel(source_ref, out_ref, sem):
+    copy = pltpu.make_async_copy(source_ref, out_ref, sem)
+    copy.start()
+    copy.wait()
+
+
+def bring(values):
+    return pl.pallas_call(
+        bring_kernel,
+        out_shape=shape(values.shape),
+        in_specs=[pl.BlockSpec(memory_space=pl.ANY)],
+        out_specs=VMEM,
+        scratch_shapes=[pltpu.SemaphoreType.DMA],
+        compiler_params=PARAMS,
+        name="bring",
+    )(values)
+
+
 def core_sum_kernel(own_ref, other_ref, keep_ref, send_ref):
     xh = lax.axis_index("xh")
     mine = pl.ds(pl.multiple_of(xh * 512, 512), 512)
@@ -376,12 +394,14 @@
     wide = lax.all_to_all(mixed.reshape(16, 2, 64, 128), CH_AXES, 0, 0)
     wide = lax.optimization_barrier(wide)
     own = call(second_norm_kernel, shape((C, 256)), [], "second_norm", (wide, sums))
+    own, late = lax.optimization_barrier((own, z2))
+    late = bring(late)
     own_out, other_out = call(
         mlp_kernel,
         [shape((C, 256), F32), shape((C, 256))],
         [],
         "channel_mlp",
-        (packed, z0, z1, z2, x0, x12, x3, own, swap(own, "core")),
+        (packed, z0, z1, late, x0, x12, x3, own, swap(own, "core")),
         limit=30 << 20,
     )
     keep, send = call(

time: 151 us -> 151 us (level)
  no operation moved by 1% of the time
where the time goes in v5:
time: 151 us; the launch traced here: 149 us
  blocking collectives  61.1 us (40%)
  starting transfers between devices  45.6 us (30%)
  waiting for transfers between devices  28.4 us (19%)
  Pallas kernels  12.2 us (8%)
    all_to_all x1, blocking collectives, per_device(): rows = lax.all_to_all(rows, LON_AXES, 0, 0)  21.5 us
    ppermute x6, starting transfers between devices, swap(): return lax.ppermute(values, axis, [(0, 1), (1, 0)])  21.1 us
    all_to_all x1, blocking collectives, per_device(): back = lax.all_to_all(back, LON_AXES, 0, 0)  16.8 us
    ppermute x2, starting transfers between devices, next_pair(): return lax.ppermute(values, ('zl', 'zh'), pairs)  15.3 us
    all_to_all x1, waiting for transfers between devices, per_device(): wide = lax.all_to_all(mixed.reshape(16, 2, 64, 128), CH_AXES, 0, 0)  13.9 us
    all_to_all x1, blocking collectives, per_device(): lax.all_to_all(lax.optimization_barrier(result), ('xl', 'zh'), 0, 0)  13.1 us
    ppermute x2, waiting for transfers between devices, next_pair(): return lax.ppermute(values, ('zl', 'zh'), pairs)  11.9 us
    all_gather x1, blocking collectives, per_device(): lax.all_gather(send, 'xh', axis=0)  9.7 us
  transfers between devices with their start and end apart: 10, of which 5 were waited for; matrix products, arithmetic and copies ran while one was open for 0% of the time, Pallas kernels for 2%

profile of v5, /device:TPU:1, one launch (start us, length us, event | category | flops | bytes accessed | tf_op | source)
XLA Modules:
  0.0 149.2 jit_solution(3184151359085206529)
XLA Ops:
  0.0 2.3 %setup.1 = (bf16[2,128,1024]{2,1,0:T(8,128)(2,1)}, f32[16,40,128]{2,1,0:T(8,128)}) custom-call(bf16[1024,256]{1,0:T(8,128)(2,1)} %up_ref.1, bf16[256,1024]{1,0:T(8,128)(2,1)} %down_ref.1, bf16[16,64,128]{2,1,0:T(8,128)(2,1)} %bitcast.13, bf16[64]{0:T(256)(128)(2,1)} %gain_ref.1), custom_call_target="tpu_custom_call" | custom-call | tf_op jit(solution)/shard_map/setup/pallas_call | solution.py:143
  2.3 4.0 %collective-permute-start.1 = (bf16[2,128,1024]{2,1,0:T(8,128)(2,1)}, bf16[2,128,1024]{2,1,0:T(8,128)(2,1)S(1)}, u32[]{:S(2)}, u32[]{:S(2)}) collective-permute-start(bf16[2,128,1024]{2,1,0:T(8,128)(2,1)} %get-tuple-element.31.refs_0_), channel_id=1, source_target_pairs={{0,4},{4,0},{1,5},{5,1},{2,6},{6,2},{3,7},{7,3},{8,12},{12,8},{9,1... | collective-permute-start | bytes 1572872 | tf_op jit(solution)/shard_map/ppermute | solution.py:327
  6.2 10.7 %collective-permute-start = (bf16[2,128,1024]{2,1,0:T(8,128)(2,1)}, bf16[2,128,1024]{2,1,0:T(8,128)(2,1)S(1)}, u32[]{:S(2)}, u32[]{:S(2)}) collective-permute-start(bf16[2,128,1024]{2,1,0:T(8,128)(2,1)} %get-tuple-element.31.refs_0_), channel_id=1, source_target_pairs={{256,1},{0,259},{257,2},{1,256},{258,3},{2,257},{259,0},{3,258},{2... | collective-permute-start | bytes 1572872 | tf_op jit(solution)/shard_map/ppermute | solution.py:335
  17.0 4.0 %all-to-all-start = ((f32[16,40,128]{2,1,0:T(8,128)}), f32[16,40,128]{2,1,0:T(8,128)S(1)}, u32[]{:S(2)}, u32[]{:S(2)}) async-start(f32[16,40,128]{2,1,0:T(8,128)} %get-tuple-element.30), calls=%async_computation | async-start | bytes 655360 | tf_op jit(solution)/shard_map/all_to_all | solution.py:343
  21.8 11.9 %collective-permute-done.refs_1_ = bf16[2,128,1024]{2,1,0:T(8,128)(2,1)S(1)} collective-permute-done((bf16[2,128,1024]{2,1,0:T(8,128)(2,1)}, bf16[2,128,1024]{2,1,0:T(8,128)(2,1)S(1)}, u32[]{:S(2)}, u32[]{:S(2)}) %collective-permute-start) | collective-permute-done | bytes 524320 | tf_op jit(solution)/shard_map/ppermute | solution.py:335
  34.4 0.8 norm_latitude.1
  35.2 5.2 %collective-permute-start.2 = (bf16[2,128,1024]{2,1,0:T(8,128)(2,1)S(1)}, bf16[2,128,1024]{2,1,0:T(8,128)(2,1)S(1)}, u32[]{:S(2)}, u32[]{:S(2)}) collective-permute-start(bf16[2,128,1024]{2,1,0:T(8,128)(2,1)S(1)} %collective-permute-done.refs_1_), channel_id=1, source_target_pairs={{0,256},{256,0},{1,257},{257,1},{2,258},{258,2},{3,259},{259,3},{4... | collective-permute-start | bytes 1572872 | tf_op jit(solution)/shard_map/ppermute | solution.py:327
  40.4 21.5 %all_to_all.25 = bf16[32,16,256]{2,1,0:T(8,128)(2,1)S(1)} all-to-all(bf16[32,16,256]{2,1,0:T(8,128)(2,1)S(1)} %get-tuple-element.36), channel_id=1, replica_groups=mesh['zl'=2,'y'=8,'core'=2,'xh'=2,'xl'=2,'zh'=4] {'zl','y','core'}, dimensions={0} | all-to-all | bytes 524288 | tf_op jit(solution)/shard_map/all_to_all | solution.py:366
  62.0 2.2 %collective-permute-start.4 = (bf16[2,2,128,1024]{3,2,1,0:T(8,128)(2,1)S(1)}, bf16[2,2,128,1024]{3,2,1,0:T(8,128)(2,1)S(1)}, u32[]{:S(2)}, u32[]{:S(2)}) collective-permute-start(bf16[2,2,128,1024]{3,2,1,0:T(8,128)(2,1)S(1)} %pad_maximum_fusion), channel_id=1, source_target_pairs={{0,4},{4,0},{1,5},{5,1},{2,6},{6,2},{3,7},{7,3},{8,12},{12,8},{9,1... | collective-permute-start | bytes 3145736 | tf_op jit(solution)/shard_map/ppermute | solution.py:327
  64.2 1.9 %spectral.1 = bf16[512,256]{1,0:T(8,128)(2,1)S(1)} custom-call(bf16[512,256]{1,0:T(8,128)(2,1)S(1)} %bitcast.19, bf16[512,512]{1,0:T(8,128)(2,1)S(1)} %copy-done.3, bf16[512,512]{1,0:T(8,128)(2,1)S(1)} %copy-done.2, bf16[432,256]{1,0:T(8,128)(2,1)S(1)} %constant_dynamic-update-slice_fusion.small_ref), custom_call_target="tpu_custom_call" | custom-call | tf_op jit(solution)/shard_map/spectral/pallas_call | solution.py:311
  66.1 4.6 %collective-permute-start.3 = (bf16[2,128,1024]{2,1,0:T(8,128)(2,1)S(1)}, bf16[2,128,1024]{2,1,0:T(8,128)(2,1)}, u32[]{:S(2)}, u32[]{:S(2)}) collective-permute-start(bf16[2,128,1024]{2,1,0:T(8,128)(2,1)S(1)} %collective-permute-done.2.refs_2_), channel_id=1, source_target_pairs={{256,1},{0,259},{257,2},{1,256},{258,3},{2,257},{259,0},{3,258},{2... | collective-permute-start | bytes 1572872 | tf_op jit(solution)/shard_map/ppermute | solution.py:335
  70.7 16.8 %all_to_all.26.rows_ref = bf16[32,16,256]{2,1,0:T(8,128)(2,1)S(1)} all-to-all(bf16[32,16,256]{2,1,0:T(8,128)(2,1)S(1)} %bitcast.20), channel_id=1, replica_groups=mesh['zl'=2,'y'=8,'core'=2,'xh'=2,'xl'=2,'zh'=4] {'zl','y','core'}, dimensions={0} | all-to-all | bytes 524288 | tf_op jit(solution)/shard_map/all_to_all | solution.py:383
  87.5 1.3 latitude_back.1
  88.9 5.3 %all-to-all-start.3 = ((bf16[16,2,64,128]{3,2,1,0:T(8,128)(2,1)}), bf16[16,2,64,128]{3,2,1,0:T(8,128)(2,1)S(1)}, u32[]{:S(2)}, u32[]{:S(2)}) async-start(bf16[16,2,64,128]{3,2,1,0:T(8,128)(2,1)} %bitcast.8), calls=%async_computation.3 | async-start | bytes 1048576 | tf_op jit(solution)/shard_map/all_to_all | solution.py:394
  94.2 3.3 %collective-permute-start.5 = (bf16[2,128,1024]{2,1,0:T(8,128)(2,1)}, bf16[2,128,1024]{2,1,0:T(8,128)(2,1)}, u32[]{:S(2)}, u32[]{:S(2)}) collective-permute-start(bf16[2,128,1024]{2,1,0:T(8,128)(2,1)} %collective-permute-done.3.source_ref), channel_id=1, source_target_pairs={{0,4},{4,0},{1,5},{5,1},{2,6},{6,2},{3,7},{7,3},{8,12},{12,8},{9,1... | collective-permute-start | bytes 1572872 | tf_op jit(solution)/shard_map/ppermute | solution.py:327
  97.5 13.9 %all-to-all-done.3.mixed_ref.wide_ref = bf16[16,2,64,128]{3,2,1,0:T(8,128)(2,1)S(1)} async-done(((bf16[16,2,64,128]{3,2,1,0:T(8,128)(2,1)}), bf16[16,2,64,128]{3,2,1,0:T(8,128)(2,1)S(1)}, u32[]{:S(2)}, u32[]{:S(2)}) %all-to-all-start.3) | async-done | bytes 524320 | tf_op jit(solution)/shard_map/all_to_all | solution.py:394
  111.9 4.3 %collective-permute-start.6 = (bf16[1024,256]{1,0:T(8,128)(2,1)S(1)}, bf16[1024,256]{1,0:T(8,128)(2,1)S(1)}, u32[]{:S(2)}, u32[]{:S(2)}) collective-permute-start(bf16[1024,256]{1,0:T(8,128)(2,1)S(1)} %second_norm.1.refs_7_), channel_id=1, source_target_pairs={{0,16},{16,0},{1,17},{17,1},{2,18},{18,2},{3,19},{19,3},{4,20},{20... | collective-permute-start | bytes 1572872 | tf_op jit(solution)/shard_map/ppermute | solution.py:327
  116.1 1.1 bring.1.refs_3_
  117.7 4.1 %channel_mlp.1 = (f32[1024,256]{1,0:T(8,128)S(1)}, bf16[1024,256]{1,0:T(8,128)(2,1)S(1)}) custom-call(bf16[2,128,1024]{2,1,0:T(8,128)(2,1)S(1)} %copy-done.1, bf16[2,128,1024]{2,1,0:T(8,128)(2,1)S(1)} %collective-permute-done.refs_1_, bf16[2,128,1024]{2,1,0:T(8,128)(2,1)S(1)} %collective-permute-done.2.refs_2_, bf16[2,128,1024]{2,1,0:T(8,128)(2,1)S(1)} %bring.1.refs_3_, ...), custom_call_target="tpu_custom_call" | custom-call | tf_op jit(solution)/shard_map/channel_mlp/pallas_call | solution.py:311
  121.8 2.3 %collective-permute-start.7 = (bf16[1024,256]{1,0:T(8,128)(2,1)S(1)}, bf16[1024,256]{1,0:T(8,128)(2,1)S(1)}, u32[]{:S(2)}, u32[]{:S(2)}) collective-permute-start(bf16[1024,256]{1,0:T(8,128)(2,1)S(1)} %get-tuple-element.52), channel_id=1, source_target_pairs={{0,16},{16,0},{1,17},{17,1},{2,18},{18,2},{3,19},{19,3},{4,20},{20... | collective-permute-start | bytes 1572872 | tf_op jit(solution)/shard_map/ppermute | solution.py:327
  124.1 1.5 %collective-permute-done.7.other_ref = bf16[1024,256]{1,0:T(8,128)(2,1)S(1)} collective-permute-done((bf16[1024,256]{1,0:T(8,128)(2,1)S(1)}, bf16[1024,256]{1,0:T(8,128)(2,1)S(1)}, u32[]{:S(2)}, u32[]{:S(2)}) %collective-permute-start.7) | collective-permute-done | bytes 524320 | tf_op jit(solution)/shard_map/ppermute | solution.py:327
  125.7 9.7 %all-gather = bf16[1024,256]{1,0:T(8,128)(2,1)S(1)} all-gather(bf16[512,256]{1,0:T(8,128)(2,1)S(1)} %get-tuple-element.54), channel_id=2, replica_groups=mesh['zl'=2,'y'=8,'core'=2,'xh'=2,'xl'=2,'zh'=4] {'xh'}, dimensions={0}, use_global_device_ids=true | all-gather | bytes 786432 | tf_op jit(solution)/shard_map/all_gather | solution.py:414
  135.5 13.1 %all_to_all.27 = bf16[8,2,64,128]{3,2,1,0:T(8,128)(2,1)S(1)} all-to-all(bf16[8,2,64,128]{3,2,1,0:T(8,128)(2,1)S(1)} %finish.1), channel_id=1, replica_groups=mesh['zl'=2,'y'=8,'core'=2,'xh'=2,'xl'=2,'zh'=4] {'xl','zh'}, dimensions={0} | all-to-all | bytes 524288 | tf_op jit(solution)/shard_map/all_to_all | solution.py:415
  148.5 0.7 copy.21
  (40 shorter events, 2.7 us)
Async XLA Ops:
  2.3 19.5 %collective-permute-start.1 = (bf16[2,128,1024]{2,1,0:T(8,128)(2,1)}, bf16[2,128,1024]{2,1,0:T(8,128)(2,1)S(1)}, u32[]{:S(2)}, u32[]{:S(2)}) collective-permute-start(bf16[2,128,1024]{2,1,0:T(8,128)(2,1)} %get-tuple-element.31.refs_0_), channel_id=1, source_target_pairs={{0,4},{4,0},{1,5},{5,1},{2,6},{6,2},{3,7},{7,3},{8,12},{12,8},{9,1... | collective-permute-start | bytes 1572872 | tf_op jit(solution)/shard_map/ppermute | solution.py:327
  6.2 27.5 %collective-permute-start = (bf16[2,128,1024]{2,1,0:T(8,128)(2,1)}, bf16[2,128,1024]{2,1,0:T(8,128)(2,1)S(1)}, u32[]{:S(2)}, u32[]{:S(2)}) collective-permute-start(bf16[2,128,1024]{2,1,0:T(8,128)(2,1)} %get-tuple-element.31.refs_0_), channel_id=1, source_target_pairs={{256,1},{0,259},{257,2},{1,256},{258,3},{2,257},{259,0},{3,258},{2... | collective-permute-start | bytes 1572872 | tf_op jit(solution)/shard_map/ppermute | solution.py:335
  16.9 4.1 %copy-start.6 = (bf16[64,256]{1,0:T(8,128)(2,1)S(1)}, bf16[64,256]{1,0:T(8,128)(2,1)}, u32[]{:S(2)}) copy-start(bf16[64,256]{1,0:T(8,128)(2,1)} %constant.15.clone) | copy-start | bytes 98308
  16.9 4.1 %copy-start.9 = (bf16[32,256]{1,0:T(8,128)(2,1)S(1)}, bf16[32,256]{1,0:T(8,128)(2,1)}, u32[]{:S(2)}) copy-start(bf16[32,256]{1,0:T(8,128)(2,1)} %constant.16.clone) | copy-start | bytes 49156
  16.9 4.1 %copy-start.8 = (bf16[32,256]{1,0:T(8,128)(2,1)S(1)}, bf16[32,256]{1,0:T(8,128)(2,1)}, u32[]{:S(2)}) copy-start(bf16[32,256]{1,0:T(8,128)(2,1)} %constant.17.clone) | copy-start | bytes 49156
  17.0 4.1 %copy-start.7 = (bf16[32,256]{1,0:T(8,128)(2,1)S(1)}, bf16[32,256]{1,0:T(8,128)(2,1)}, u32[]{:S(2)}) copy-start(bf16[32,256]{1,0:T(8,128)(2,1)} %constant.18.clone) | copy-start | bytes 49156
  17.0 4.1 %copy-start.4 = (bf16[2,64,64]{2,1,0:T(8,128)(2,1)S(1)}, bf16[2,64,64]{2,1,0:T(8,128)(2,1)}, u32[]{:S(2)}) copy-start(bf16[2,64,64]{2,1,0:T(8,128)(2,1)} %param.15) | copy-start | bytes 49156
  17.0 4.1 %copy-start.5 = (bf16[2,64,64]{2,1,0:T(8,128)(2,1)S(1)}, bf16[2,64,64]{2,1,0:T(8,128)(2,1)}, u32[]{:S(2)}) copy-start(bf16[2,64,64]{2,1,0:T(8,128)(2,1)} %param.16) | copy-start | bytes 49156
  17.0 17.4 %all-to-all-start = ((f32[16,40,128]{2,1,0:T(8,128)}), f32[16,40,128]{2,1,0:T(8,128)S(1)}, u32[]{:S(2)}, u32[]{:S(2)}) async-start(f32[16,40,128]{2,1,0:T(8,128)} %get-tuple-element.30), calls=%async_computation | async-start | bytes 655360 | tf_op jit(solution)/shard_map/all_to_all | solution.py:343
  21.0 13.4 %copy-start = (bf16[128,16,64]{0,2,1:T(8,128)(2,1)S(1)}, bf16[128,16,64]{0,2,1:T(8,128)(2,1)}, u32[]{:S(2)}) copy-start(bf16[128,16,64]{0,2,1:T(8,128)(2,1)} %param.13) | copy-start | bytes 786436
  21.1 0.7 copy-start.10
  35.2 26.7 %collective-permute-start.2 = (bf16[2,128,1024]{2,1,0:T(8,128)(2,1)S(1)}, bf16[2,128,1024]{2,1,0:T(8,128)(2,1)S(1)}, u32[]{:S(2)}, u32[]{:S(2)}) collective-permute-start(bf16[2,128,1024]{2,1,0:T(8,128)(2,1)S(1)} %collective-permute-done.refs_1_), channel_id=1, source_target_pairs={{0,256},{256,0},{1,257},{257,1},{2,258},{258,2},{3,259},{259,3},{4... | collective-permute-start | bytes 1572872 | tf_op jit(solution)/shard_map/ppermute | solution.py:327
  61.9 2.3 %copy-start.2 = (bf16[512,512]{1,0:T(8,128)(2,1)S(1)}, bf16[512,512]{1,0:T(8,128)(2,1)}, u32[]{:S(2)}) copy-start(bf16[512,512]{1,0:T(8,128)(2,1)} %constant.20.clone.inverse_ref) | copy-start | bytes 1572868
  61.9 2.3 %copy-start.3 = (bf16[512,512]{1,0:T(8,128)(2,1)S(1)}, bf16[512,512]{1,0:T(8,128)(2,1)}, u32[]{:S(2)}) copy-start(bf16[512,512]{1,0:T(8,128)(2,1)} %constant.19.clone.lon_ref) | copy-start | bytes 1572868
  62.0 25.5 %collective-permute-start.4 = (bf16[2,2,128,1024]{3,2,1,0:T(8,128)(2,1)S(1)}, bf16[2,2,128,1024]{3,2,1,0:T(8,128)(2,1)S(1)}, u32[]{:S(2)}, u32[]{:S(2)}) collective-permute-start(bf16[2,2,128,1024]{3,2,1,0:T(8,128)(2,1)S(1)} %pad_maximum_fusion), channel_id=1, source_target_pairs={{0,4},{4,0},{1,5},{5,1},{2,6},{6,2},{3,7},{7,3},{8,12},{12,8},{9,1... | collective-permute-start | bytes 3145736 | tf_op jit(solution)/shard_map/ppermute | solution.py:327
  66.1 21.4 %collective-permute-start.3 = (bf16[2,128,1024]{2,1,0:T(8,128)(2,1)S(1)}, bf16[2,128,1024]{2,1,0:T(8,128)(2,1)}, u32[]{:S(2)}, u32[]{:S(2)}) collective-permute-start(bf16[2,128,1024]{2,1,0:T(8,128)(2,1)S(1)} %collective-permute-done.2.refs_2_), channel_id=1, source_target_pairs={{256,1},{0,259},{257,2},{1,256},{258,3},{2,257},{259,0},{3,258},{2... | collective-permute-start | bytes 1572872 | tf_op jit(solution)/shard_map/ppermute | solution.py:335
  88.9 22.4 %all-to-all-start.3 = ((bf16[16,2,64,128]{3,2,1,0:T(8,128)(2,1)}), bf16[16,2,64,128]{3,2,1,0:T(8,128)(2,1)S(1)}, u32[]{:S(2)}, u32[]{:S(2)}) async-start(bf16[16,2,64,128]{3,2,1,0:T(8,128)(2,1)} %bitcast.8), calls=%async_computation.3 | async-start | bytes 1048576 | tf_op jit(solution)/shard_map/all_to_all | solution.py:394
  94.2 23.0 %collective-permute-start.5 = (bf16[2,128,1024]{2,1,0:T(8,128)(2,1)}, bf16[2,128,1024]{2,1,0:T(8,128)(2,1)}, u32[]{:S(2)}, u32[]{:S(2)}) collective-permute-start(bf16[2,128,1024]{2,1,0:T(8,128)(2,1)} %collective-permute-done.3.source_ref), channel_id=1, source_target_pairs={{0,4},{4,0},{1,5},{5,1},{2,6},{6,2},{3,7},{7,3},{8,12},{12,8},{9,1... | collective-permute-start | bytes 1572872 | tf_op jit(solution)/shard_map/ppermute | solution.py:327
  111.9 5.8 %copy-start.1 = (bf16[2,128,1024]{2,1,0:T(8,128)(2,1)S(1)}, bf16[2,128,1024]{2,1,0:T(8,128)(2,1)}, u32[]{:S(2)}) copy-start(bf16[2,128,1024]{2,1,0:T(8,128)(2,1)} %get-tuple-element.31.refs_0_) | copy-start | bytes 1572868
  111.9 5.8 %collective-permute-start.6 = (bf16[1024,256]{1,0:T(8,128)(2,1)S(1)}, bf16[1024,256]{1,0:T(8,128)(2,1)S(1)}, u32[]{:S(2)}, u32[]{:S(2)}) collective-permute-start(bf16[1024,256]{1,0:T(8,128)(2,1)S(1)} %second_norm.1.refs_7_), channel_id=1, source_target_pairs={{0,16},{16,0},{1,17},{17,1},{2,18},{18,2},{3,19},{19,3},{4,20},{20... | collective-permute-start | bytes 1572872 | tf_op jit(solution)/shard_map/ppermute | solution.py:327
  121.8 3.8 %collective-permute-start.7 = (bf16[1024,256]{1,0:T(8,128)(2,1)S(1)}, bf16[1024,256]{1,0:T(8,128)(2,1)S(1)}, u32[]{:S(2)}, u32[]{:S(2)}) collective-permute-start(bf16[1024,256]{1,0:T(8,128)(2,1)S(1)} %get-tuple-element.52), channel_id=1, source_target_pairs={{0,16},{16,0},{1,17},{17,1},{2,18},{18,2},{3,19},{19,3},{4,20},{20... | collective-permute-start | bytes 1572872 | tf_op jit(solution)/shard_map/ppermute | solution.py:327
